TPU v7x, 32 devices: a whole 2x2x4 slice. The times are simulated.
32 devices in a mesh: crops: 2 (over x), rows: 8 (over z, y), cols: 2 (over core).
Axes of the slice: x: 2, y: 2, z: 4, core: 2. Of those that a mesh axis runs over, the one named last changes fastest.
Arguments:
- pair: bfloat16 [1024, 512, 128], P(('crops', 'rows'), 'cols'), parts along dimension 0, may hold values from -6 to 6
- token_mask: int32 [1024], P('crops'), parts along dimension 0, may hold values 0 or 1
- in_gain: float32 [128], replicated, may hold values from 0.25 to 1.75
- left_proj: bfloat16 [128, 128], replicated, may hold values from -0.5 to 0.5
- left_gate: bfloat16 [128, 128], replicated, may hold values from -0.5 to 0.5
- right_proj: bfloat16 [128, 128], replicated, may hold values from -0.5 to 0.5
- right_gate: bfloat16 [128, 128], replicated, may hold values from -0.5 to 0.5
- out_gate: bfloat16 [128, 128], replicated, may hold values from -0.5 to 0.5
- out_gain: float32 [128], replicated, may hold values from 0.25 to 1.75
- out_proj: bfloat16 [128, 128], replicated, may hold values from -0.5 to 0.5
Outputs:
- pair_out: bfloat16 [1024, 512, 128], P(('crops', 'rows'), 'cols'), parts along dimension 0
There are 2 independent parts, one for each index of `crops`. A program takes and returns all parts, laid end to end along the dimension named above; an argument that names none is the same for every part. Nothing has to cross between parts.
Inputs may be any that keep to these rules, and one draw needn't show every extreme that they name: `token_mask`: 1 marks a real token, 0 a padding position.
All inputs are finite; a program needn't handle non-finite values.
Results may differ from a plain program's by a relative error of at most 0.0049.
Values may be sent and summed in bfloat16 or wider, within the bound.
A program may use at most 192 MiB of HBM per device.

v0:
```python
import jax
import jax.numpy as jnp
from jax import lax
from jax.sharding import PartitionSpec as P


def norm_last(values, gains):
    average = jnp.mean(values, axis=-1, keepdims=True)
    centred = values - average
    spread = jnp.mean(centred * centred, axis=-1, keepdims=True)
    return centred * lax.rsqrt(spread + 1e-05) * gains


def norm_first(values, gains):
    average = jnp.mean(values, axis=0, keepdims=True)
    centred = values - average
    spread = jnp.mean(centred * centred, axis=0, keepdims=True)
    return centred * lax.rsqrt(spread + 1e-05) * gains[:, None, None]


def turn_pair(tile_block, n_rows, n_cols):
    stripes = lax.all_to_all(tile_block, "cols", split_axis=1, concat_axis=0, tiled=True)
    arrived = lax.all_to_all(stripes, "rows", split_axis=0, concat_axis=1, tiled=True)
    row_width = arrived.shape[0]
    stripe_width = stripes.shape[1]
    channels = arrived.shape[2]
    row_group = n_rows // n_cols
    sectioned = arrived.reshape(row_width, n_cols, row_group, 1, stripe_width, channels)
    regrouped = lax.all_to_all(sectioned, "cols", split_axis=1, concat_axis=3, tiled=True)
    return regrouped.reshape(row_width, row_group * n_cols * stripe_width, channels)


def body(
    pair,
    token_mask,
    in_gain,
    left_proj,
    left_gate,
    right_proj,
    right_gate,
    out_gate,
    out_gain,
    out_proj,
):
    n_rows = lax.axis_size("rows")
    n_cols = lax.axis_size("cols")
    rows_tile = pair.shape[0]
    cols_tile = pair.shape[1]
    row_at = lax.axis_index("rows")
    col_at = lax.axis_index("cols")
    mask_values = token_mask.astype(jnp.float32)
    mask_rows = lax.dynamic_slice_in_dim(mask_values, row_at * rows_tile, rows_tile)
    mask_cols = lax.dynamic_slice_in_dim(mask_values, col_at * cols_tile, cols_tile)
    pair_mask = (mask_rows[:, None] * mask_cols[None, :])[None, :, :]
    normed = norm_last(pair.astype(jnp.float32), in_gain).astype(jnp.bfloat16)

    def gated(w_proj, w_gate):
        projected = jnp.einsum("xkd,dh->hxk", normed, w_proj, preferred_element_type=jnp.float32)
        gate_logits = jnp.einsum("xkd,dh->hxk", normed, w_gate, preferred_element_type=jnp.float32)
        return (jax.nn.sigmoid(gate_logits) * projected * pair_mask).astype(jnp.bfloat16)

    left_side = gated(left_proj, left_gate)
    right_side = gated(right_proj, right_gate)
    resident, shipped = (left_side, right_side)
    partial_value = jnp.einsum(
        "hxk,hyk->hxy",
        resident,
        lax.all_gather(shipped, "rows", axis=1, tiled=True),
        preferred_element_type=jnp.float32,
    )
    summed = lax.psum_scatter(partial_value, "cols", scatter_dimension=2, tiled=True)
    combined_norm = norm_first(summed, out_gain).astype(jnp.bfloat16)
    gate_values = jax.nn.sigmoid(
        jnp.einsum("ijd,dc->jic", normed, out_gate, preferred_element_type=jnp.float32)
    )
    update = jnp.einsum("hij,hd->jid", combined_norm, out_proj, preferred_element_type=jnp.float32)
    swapped = jnp.transpose(pair, (1, 0, 2)).astype(jnp.float32)
    result = (swapped + gate_values * update).astype(jnp.bfloat16)
    return turn_pair(result, n_rows, n_cols)


def solution(mesh):
    return jax.shard_map(
        body,
        mesh=mesh,
        in_specs=(
            P(("crops", "rows"), "cols", None),
            P("crops"),
            P(),
            P(),
            P(),
            P(),
            P(),
            P(),
            P(),
            P(),
        ),
        out_specs=P(("crops", "rows"), "cols", None),
        check_vma=False,
    )
```

profile of v0, /device:TPU:1, one launch (start us, length us, event | category | flops | bytes accessed | tf_op | source)
XLA Modules:
  0.0 892.4 jit_solution(14389397120393271051)
XLA Ops:
  6.5 0.7 convert_element_type.31
  7.3 0.1 dynamic_slice.6
  7.3 0.1 dynamic_slice.7
  7.4 3.5 convert_reduce_fusion
  10.9 6.0 fusion.4
  16.9 0.1 add_rsqrt_fusion.1
  17.0 4.8 fusion.15
  21.8 8.8 fusion.11
  30.6 6.4 copy.25
  37.1 0.0 all-gather.2.cloned.1.call-update
  37.1 0.2 reduce-scatter.2.cloned.1.call-start
  37.4 8.2 fusion.18
  45.6 8.8 fusion.10
  54.4 6.9 copy.26
  61.2 615.8 %all-gather.2.cloned.1.call-done = bf16[128,512,256]{2,0,1:T(8,128)(2,1)} async-done(((bf16[128,64,256]{2,0,1:T(8,128)(2,1)}), bf16[128,512,256]{2,0,1:T(8,128)(2,1)}) %all-gather.2.cloned.1.call-update) | async-done | bytes 33554448 | tf_op jit(solution)/shard_map/all_gather | solution.py:68
  677.1 36.1 %fusion = f32[128,64,512]{2,1,0:T(8,128)} fusion(bf16[128,64,256]{2,1,0:T(8,128)(2,1)} %copy.26, bf16[128,512,256]{2,0,1:T(8,128)(2,1)} %all-gather.2.cloned.1.call-done), kind=kOutput, calls=%fused_computation | convolution fusion | flops 2147483648 | bytes 54525952 | tf_op jit(solution)/shard_map/hxk,hyk->hxy/dot_general | solution.py:65
  713.2 0.0 reduce-scatter.2.cloned.1.call-update
  713.2 0.0 copy-start.9
  713.2 26.9 %reduce-scatter.2.cloned.1.call-done = f32[128,64,256]{2,1,0:T(8,128)} async-done(((f32[128,64,512]{2,1,0:T(8,128)}), f32[128,64,256]{2,1,0:T(8,128)}) %reduce-scatter.2.cloned.1.call-update) | async-done | bytes 8388624 | tf_op jit(solution)/shard_map/reduce_scatter | solution.py:71
  740.1 3.8 reduce_sum.38
  743.9 4.4 multiply_reduce_fusion
  748.4 1.3 copy-done.2
  749.7 1.0 multiply_convert_fusion.2
  750.8 4.9 fusion.8
  755.7 8.0 fusion.12
  763.6 7.0 all_to_all.48
  770.6 2.7 copy.29
  773.3 97.6 %all_to_all.49 = bf16[512,32,128]{2,1,0:T(8,128)(2,1)S(1)} all-to-all(bf16[512,32,128]{2,1,0:T(8,128)(2,1)S(1)} %bitcast.39), channel_id=1, replica_groups=mesh['crops'=2,'rows'=8,'cols'=2] {'rows'}, dimensions={0} | all-to-all | bytes 8388608 | tf_op jit(solution)/shard_map/all_to_all | solution.py:23
  870.9 1.3 copy.30
  872.2 1.6 copy.31
  873.8 8.5 all_to_all.50
  882.3 3.2 copy.32
  (28 shorter events, 0.1 us)
Async XLA Ops:
  6.5 10.5 %copy-start = (bf16[128,128]{1,0:T(8,128)(2,1)S(1)}, bf16[128,128]{1,0:T(8,128)(2,1)}, u32[]{:S(2)}) copy-start(bf16[128,128]{1,0:T(8,128)(2,1)} %param.16) | copy-start | bytes 98308
  6.5 10.5 %copy-start.8 = (f32[128]{0:T(128)S(1)}, f32[128]{0:T(128)}, u32[]{:S(2)}) copy-start(f32[128]{0:T(128)} %param.12) | copy-start | bytes 1540
  6.5 670.5 %all-gather.2.cloned.1.call-start = ((), (), s32[]{:S(2)}) async-start(), calls=%async_computation.4 | async-start | bytes 37748736 | tf_op jit(solution)/shard_map/all_gather | solution.py:68
  7.3 9.8 %copy-start.3 = (bf16[64,256,128]{2,1,0:T(8,128)(2,1)S(1)}, bf16[64,256,128]{2,1,0:T(8,128)(2,1)}, u32[]{:S(2)}) copy-start(bf16[64,256,128]{2,1,0:T(8,128)(2,1)} %param.10) | copy-start | bytes 12582916
  10.9 10.9 %copy-start.10 = (bf16[128,128]{1,0:T(8,128)(2,1)S(1)}, bf16[128,128]{1,0:T(8,128)(2,1)}, u32[]{:S(2)}) copy-start(bf16[128,128]{1,0:T(8,128)(2,1)} %param.15) | copy-start | bytes 98308
  30.6 6.7 copy-start.6
  37.1 8.5 copy-start.11
  37.1 703.0 %reduce-scatter.2.cloned.1.call-start = ((), (), s32[]{:S(2)}) async-start(), calls=%async_computation.5 | async-start | bytes 25165824 | tf_op jit(solution)/shard_map/reduce_scatter | solution.py:71
  37.3 8.2 copy-start.4
  713.2 35.2 %copy-start.9 = (f32[128]{0:T(128)S(1)}, f32[128]{0:T(128)}, u32[]{:S(2)}) copy-start(f32[128]{0:T(128)} %param.18) | copy-start | bytes 1540
  743.9 5.8 copy-start.2
  748.4 2.4 copy-start.7
  750.7 4.9 copy-start.5
  750.8 4.9 copy-start.12
  872.2 13.4 %copy-start.1 = (bf16[128,128]{1,0:T(8,128)(2,1)S(1)}, bf16[128,128]{1,0:T(8,128)(2,1)}, u32[]{:S(2)}) copy-start(bf16[128,128]{1,0:T(8,128)(2,1)} %param.16) | copy-start | bytes 98308
Sparse Core Ops, SparseCore 0:
  37.2 639.7 all-gather.1
  713.3 26.6 reduce-scatter.1
where the time goes:
time: 893 us; the launch traced here: 892 us
  waiting for transfers between devices  643 us (72%)
  blocking collectives  113 us (13%)
  matrix products  79.5 us (9%)
  local copies, waits for them, and re-layouts  23.6 us (3%)
  other arithmetic  19.6 us (2%)
  between operations  13.6 us (2%)
    all_gather x1, waiting for transfers between devices, body(): lax.all_gather(shipped, 'rows', axis=1, tiled=True)  616 us
    all_to_all x1, blocking collectives, turn_pair(): lax.all_to_all(stripes, 'rows', split_axis=0, concat_axis=1, tiled=True)  97.6 us
    dot_general x1, matrix products, body(): jnp.einsum('hxk,hyk->hxy', resident, lax.all_gather(shipped, 'rows', axis...  36.1 us
    reduce_scatter x1, waiting for transfers between devices, body(): lax.psum_scatter(partial_value, 'cols', scatter_dimension=2, tiled=True)  26.9 us
  transfers between devices with their start and end apart: 2, of which 2 were waited for; matrix products, arithmetic and copies ran while one was open for 3% of the time, Pallas kernels for 0%

commit v1 on v0

v1 whole, which is shorter than its diff:
```python
import jax
import jax.numpy as jnp
from jax import lax
from jax.sharding import PartitionSpec as P

CHUNKS = 2


def norm_last(values, gains):
    average = jnp.mean(values, axis=-1, keepdims=True)
    centred = values - average
    spread = jnp.mean(centred * centred, axis=-1, keepdims=True)
    return centred * lax.rsqrt(spread + 1e-05) * gains


def norm_first(values, gains):
    average = jnp.mean(values, axis=0, keepdims=True)
    centred = values - average
    spread = jnp.mean(centred * centred, axis=0, keepdims=True)
    return centred * lax.rsqrt(spread + 1e-05) * gains[:, None, None]


def body(
    pair,
    token_mask,
    in_gain,
    left_proj,
    left_gate,
    right_proj,
    right_gate,
    out_gate,
    out_gain,
    out_proj,
):
    n_rows = lax.axis_size("rows")
    n_cols = lax.axis_size("cols")
    assert n_rows % 4 == 0 and n_cols == 2
    n_pairs = n_rows // 2
    half_pairs = n_pairs // 2
    rows_tile, cols_tile, channels = pair.shape
    row_at = lax.axis_index("rows")
    col_at = lax.axis_index("cols")
    pair_at, side_at = row_at // 2, row_at % 2

    mask_values = token_mask.astype(jnp.float32)
    mask_cols = lax.dynamic_slice_in_dim(mask_values, col_at * cols_tile, cols_tile)

    def along(block, step):
        return lax.ppermute(
            block, "rows", [(r, (r + 2 * step) % n_rows) for r in range(n_rows)]
        )

    def across(block):
        return lax.ppermute(block, "rows", [(r, r ^ 1) for r in range(n_rows)])

    def sibling(block):
        return lax.ppermute(block, "cols", [(0, 1), (1, 0)])

    def after(value, *others):
        return lax.optimization_barrier((value, *others))[0]

    order = [d + h * half_pairs for d in range(half_pairs) for h in (0, 1)]
    chunk_rows = rows_tile // CHUNKS
    own = [pair[n * chunk_rows : (n + 1) * chunk_rows] for n in range(CHUNKS)]
    mine, other = {}, {}
    z_queue, y_queue = [], []
    for d in order:
        for n in range(CHUNKS):
            if d == 0:
                mine[d, n] = own[n]
            else:
                source = own[n] if len(z_queue) < 2 else after(own[n], z_queue[-2])
                mine[d, n] = along(source, d)
                z_queue.append(mine[d, n])
            source = mine[d, n] if len(y_queue) < 2 else after(mine[d, n], y_queue[-2])
            other[d, n] = across(source)
            y_queue.append(other[d, n])

    def gated(normed, w_proj, w_gate, pair_mask):
        projected = jnp.einsum("xkd,dh->hxk", normed, w_proj, preferred_element_type=jnp.float32)
        gate_logits = jnp.einsum("xkd,dh->hxk", normed, w_gate, preferred_element_type=jnp.float32)
        return (jax.nn.sigmoid(gate_logits) * projected * pair_mask[None]).astype(jnp.bfloat16)

    def normalise(values):
        return norm_last(values.astype(jnp.float32), in_gain).astype(jnp.bfloat16)

    mask_rows = lax.dynamic_slice_in_dim(mask_values, row_at * rows_tile, rows_tile)
    right_side = gated(
        normalise(pair), right_proj, right_gate, mask_rows[:, None] * mask_cols[None, :]
    )
    width = 2 * rows_tile

    def block_of(d):
        held = jnp.concatenate([mine[d, n] for n in range(CHUNKS)], axis=0)
        swapped = jnp.concatenate([other[d, n] for n in range(CHUNKS)], axis=0)
        first = jnp.where(side_at == 0, held, swapped)
        second = jnp.where(side_at == 0, swapped, held)
        return jnp.concatenate([first, second], axis=0)

    def source_pair(d):
        return lax.rem(pair_at - d + n_pairs, n_pairs)

    def product(block, d):
        rows_mask = lax.dynamic_slice_in_dim(mask_values, source_pair(d) * width, width)
        left_side = gated(
            normalise(block), left_proj, left_gate, rows_mask[:, None] * mask_cols[None, :]
        )
        return jnp.einsum("hxk,hyk->hyx", left_side, right_side, preferred_element_type=jnp.float32)

    column_at = lax.rem(row_at * rows_tile, cols_tile)
    column_core = (row_at * rows_tile) // cols_tile

    out = jnp.zeros((rows_tile, cols_tile, channels), jnp.bfloat16)
    for d in range(half_pairs):
        near, far = block_of(d), block_of(d + half_pairs)
        keep_near = source_pair(d) // half_pairs == col_at
        near_pair = lax.dynamic_slice_in_dim(near, column_at, rows_tile, 1)
        far_pair = lax.dynamic_slice_in_dim(far, column_at, rows_tile, 1)
        kept_pair = jnp.where(keep_near, near_pair, far_pair)
        got_pair = sibling(jnp.where(keep_near, far_pair, near_pair))
        turned = jnp.where(column_core == col_at, kept_pair, got_pair)
        gate_values = jax.nn.sigmoid(
            jnp.einsum(
                "ijd,dc->jic", normalise(turned), out_gate, preferred_element_type=jnp.float32
            )
        )
        near_sum, far_sum = product(near, d), product(far, d + half_pairs)
        got_sum = sibling(jnp.where(keep_near, far_sum, near_sum).astype(jnp.bfloat16))
        combined = jnp.where(keep_near, near_sum, far_sum) + got_sum.astype(jnp.float32)
        combined_norm = norm_first(combined, out_gain).astype(jnp.bfloat16)
        update = jnp.einsum(
            "hji,hd->jid", combined_norm, out_proj, preferred_element_type=jnp.float32
        )
        swapped = jnp.transpose(turned, (1, 0, 2)).astype(jnp.float32)
        result = (swapped + gate_values * update).astype(jnp.bfloat16)
        place = lax.rem(pair_at - d + n_pairs, half_pairs)
        out = lax.dynamic_update_slice(out, result, (0, place * width, 0))
    return out


def solution(mesh):
    return jax.shard_map(
        body,
        mesh=mesh,
        in_specs=(
            P(("crops", "rows"), "cols", None),
            P("crops"),
            P(),
            P(),
            P(),
            P(),
            P(),
            P(),
            P(),
            P(),
        ),
        out_specs=P(("crops", "rows"), "cols", None),
        check_vma=False,
    )
```

time: 893 us -> 769 us (0.86); the launches traced: 892 us -> 758 us
  waiting for transfers between devices: 643 us -> 182 us
  local copies, waits for them, and re-layouts: 23.6 us -> 197 us
  other arithmetic: 19.6 us -> 154 us
  matrix products: 79.5 us -> 206 us
  blocking collectives: 113 us -> 0 us
  starting transfers between devices: 0.22 us -> 17.8 us
  between operations: 13.6 us -> 1.12 us
    all_gather x1 -> x0, waiting for transfers between devices: 616 us -> none  [body(): lax.all_gather(shipped, 'rows', axis=1, tiled=True)]
    ppermute x0 -> x18, waiting for transfers between devices: none -> 182 us  [the longest x6 181 us: along(): lax.ppermute(block, 'rows', [(r, (r + 2 * step) % n_rows) for r in range(...]
    dot_general x0 -> x8, local copies, waits for them, and re-layouts: none -> 142 us  [the longest x4 71 us: gated(): jnp.einsum('xkd,dh->hxk', normed, w_gate, preferred_element_type=jnp.floa...]
    all_to_all x3 -> x0, blocking collectives: 113 us -> none  [the longest x1 97.6 us: turn_pair(): lax.all_to_all(stripes, 'rows', split_axis=0, concat_axis=1, tiled=True)]
    dot_general x2 -> x5, matrix products: 17.6 us -> 67.4 us  [gated(): jnp.einsum('xkd,dh->hxk', normed, w_proj, preferred_element_type=jnp.floa...]
    reduce_sum x1 -> x7, other arithmetic: 5.99 us -> 55.1 us  [norm_last(): spread = jnp.mean(centred * centred, axis=-1, keepdims=True)]
    dot_general x2 -> x5, matrix products: 12.9 us -> 59.1 us  [gated(): jnp.einsum('xkd,dh->hxk', normed, w_gate, preferred_element_type=jnp.floa...]
    dot_general x3 -> x8, matrix products: 49 us -> 79.8 us  [the longest x4 67.1 us: product(): jnp.einsum('hxk,hyk->hyx', left_side, right_side, preferred_element_type=...]
  transfers between devices with their start and end apart: 2 -> 18, of which waited for: 2 -> 2; matrix products, arithmetic and copies ran while one was open for 3% -> 64% of each run, Pallas kernels for 0% -> 0%
where the time goes in v1:
time: 769 us; the launch traced here: 758 us
  matrix products  206 us (27%)
  local copies, waits for them, and re-layouts  197 us (26%)
  waiting for transfers between devices  182 us (24%)
  other arithmetic  154 us (20%)
  starting transfers between devices  17.8 us (2%)
    ppermute x6, waiting for transfers between devices, along(): lax.ppermute(block, 'rows', [(r, (r + 2 * step) % n_rows) for r in range(...  181 us
    dot_general x4, local copies, waits for them, and re-layouts, gated(): jnp.einsum('xkd,dh->hxk', normed, w_gate, preferred_element_type=jnp.floa...  71 us
    dot_general x4, local copies, waits for them, and re-layouts, gated(): jnp.einsum('xkd,dh->hxk', normed, w_proj, preferred_element_type=jnp.floa...  71 us
    dot_general x5, matrix products, gated(): jnp.einsum('xkd,dh->hxk', normed, w_proj, preferred_element_type=jnp.floa...  67.4 us
    dot_general x4, matrix products, product(): jnp.einsum('hxk,hyk->hyx', left_side, right_side, preferred_element_type=...  67.1 us
    dot_general x5, matrix products, gated(): jnp.einsum('xkd,dh->hxk', normed, w_gate, preferred_element_type=jnp.floa...  59.1 us
    reduce_sum x7, other arithmetic, norm_last(): spread = jnp.mean(centred * centred, axis=-1, keepdims=True)  55.1 us
    reduce_sum x7, other arithmetic, norm_last(): average = jnp.mean(values, axis=-1, keepdims=True)  32.3 us
  transfers between devices with their start and end apart: 18, of which 2 were waited for; matrix products, arithmetic and copies ran while one was open for 64% of the time, Pallas kernels for 0%

profile of v1, /device:TPU:1, one launch (start us, length us, event | category | flops | bytes accessed | tf_op | source)
XLA Modules:
  0.0 758.3 jit_solution(11270982458203152957)
XLA Ops:
  22.5 7.8 %fusion.65 = f32[64,256,128]{2,1,0:T(8,128)} fusion(bf16[64,256,128]{2,1,0:T(8,128)(2,1)S(1)} %copy-done.1, f32[128]{0:T(128)S(1)} %copy-done.34, f32[64,256]{1,0:T(8,128)S(1)} %add_rsqrt_fusion.4, f32[64,256]{1,0:T(8,128)S(1)} %broadcast_multiply_fusion.9, bf16[128,128]{1,0:T(8,128)(2,1)S(1)} %copy-done.33), kind=kOutput, calls=%fused_computation.107 | convolution fusion | flops 547356672 | bytes 12747264 | tf_op jit(solution)/shard_map/xkd,dh->hxk/dot_general | solution.py:81
  30.4 11.9 %fusion.63 = bf16[128,64,256]{0,2,1:T(8,128)(2,1)} fusion(f32[64,256]{1,0:T(8,128)S(1)} %broadcast_multiply_fusion.8, f32[64,256,128]{2,1,0:T(8,128)} %fusion.65, bf16[64,256,128]{2,1,0:T(8,128)(2,1)} %param.10, f32[128]{0:T(128)S(1)} %copy-done.34, f32[64,256]{1,0:T(8,128)S(1)} %add_rsqrt_fusion.4, f32[64,256]{1,0:T(8,128)S(1)} %broadcast_multiply_fusion.9, ...), kind=kOutput, calls=%fused_computation.106 | convolution fusion | flops 559939584 | bytes 17007104 | tf_op jit(solution)/shard_map/xkd,dh->hxk/dot_general | solution.py:80
  42.4 6.8 copy.15
  50.1 94.0 %collective-permute-done.2 = bf16[32,256,128]{2,0,1:T(8,128)(2,1)} collective-permute-done((bf16[32,256,128]{2,0,1:T(8,128)(2,1)}, bf16[32,256,128]{2,0,1:T(8,128)(2,1)}, u32[]{:S(2)}, u32[]{:S(2)}) %collective-permute-start.2) | collective-permute-done | bytes 2097184 | tf_op jit(solution)/shard_map/ppermute | solution.py:49
  146.5 87.5 %collective-permute-done.3 = bf16[32,256,128]{2,0,1:T(8,128)(2,1)} collective-permute-done((bf16[32,256,128]{2,0,1:T(8,128)(2,1)}, bf16[32,256,128]{2,0,1:T(8,128)(2,1)}, u32[]{:S(2)}, u32[]{:S(2)}) %collective-permute-start.3) | collective-permute-done | bytes 2097184 | tf_op jit(solution)/shard_map/ppermute | solution.py:49
  237.7 11.1 %broadcast_select_fusion.7 = (bf16[64,256,128]{2,0,1:T(8,128)(2,1)}, bf16[64,256,128]{2,0,1:T(8,128)(2,1)}) fusion(bf16[64,256,128]{2,0,1:T(8,128)(2,1)S(1)} %constant_dynamic-update-slice_fusion, pred[]{:T(512)S(6)} %eq.12, bf16[64,256,128]{2,1,0:T(8,128)(2,1)S(1)} %copy-done.2), kind=kLoop, calls=%fused_computation.105 | loop fusion | flops 4194304 | bytes 16777216 | tf_op jit(solution)/shard_map/jit(_where)/select_n | solution.py:96
  254.6 11.0 %fusion.17 = f32[128,256]{0,1:T(8,128)S(1)} fusion(f32[128,256]{0,1:T(8,128)S(1)} %broadcast_multiply_fusion.7, bf16[64,256,128]{2,0,1:T(8,128)(2,1)} %get-tuple-element.38, bf16[64,256,128]{2,0,1:T(8,128)(2,1)} %get-tuple-element.37), kind=kLoop, calls=%fused_computation.25 | loop fusion | flops 29327360 | bytes 8650752 | tf_op jit(solution)/shard_map/reduce_sum | solution.py:12
  265.7 12.8 %fusion.35 = f32[128,256,128]{2,0,1:T(8,128)} fusion(f32[128]{0:T(128)S(1)} %copy-done.34, f32[128,256]{0,1:T(8,128)S(1)} %add_rsqrt_fusion.3, f32[128,256]{0,1:T(8,128)S(1)} %broadcast_multiply_fusion.7, bf16[128,128]{1,0:T(8,128)(2,1)S(1)} %copy-done, bf16[64,256,128]{2,0,1:T(8,128)(2,1)S(1)} %copy-done.5, bf16[64,256,128]{2,0,1:T(8,128)(2,1)S(1)} %copy-done.3), kind=kOutput, calls=%fused_computation.67 | convolution fusion | flops 1107296256 | bytes 25461248 | tf_op jit(solution)/shard_map/xkd,dh->hxk/dot_general | solution.py:81
  278.5 17.8 %copy.29 = f32[128,256,128]{1,0,2:T(8,128)} copy(f32[128,256,128]{2,0,1:T(8,128)} %fusion.35) | data formatting | bytes 33554432 | tf_op jit(solution)/shard_map/xkd,dh->hxk/dot_general | solution.py:81
  296.3 15.0 %fusion.33 = f32[128,256,128]{2,0,1:T(8,128)} fusion(f32[128]{0:T(128)S(1)} %copy-done.34, f32[128,256]{0,1:T(8,128)S(1)} %add_rsqrt_fusion.3, f32[128,256]{0,1:T(8,128)S(1)} %broadcast_multiply_fusion.7, bf16[128,128]{1,0:T(8,128)(2,1)S(1)} %copy-done.37, bf16[64,256,128]{2,0,1:T(8,128)(2,1)} %get-tuple-element.38, bf16[64,256,128]{2,0,1:T(8,128)(2,1)} %get-tuple-element.37), kind=kOutput, calls=%fused_computation.66 | convolution fusion | flops 1107296256 | bytes 25461248 | tf_op jit(solution)/shard_map/xkd,dh->hxk/dot_general | solution.py:80
  311.2 17.8 %copy.30 = f32[128,256,128]{1,0,2:T(8,128)} copy(f32[128,256,128]{2,0,1:T(8,128)} %fusion.33) | data formatting | bytes 33554432 | tf_op jit(solution)/shard_map/xkd,dh->hxk/dot_general | solution.py:80
  333.3 17.0 %fusion.31 = f32[128,64,128]{2,1,0:T(8,128)} fusion(bf16[128,64,256]{2,1,0:T(8,128)(2,1)} %copy.15, f32[128,256,128]{1,0,2:T(8,128)} %copy.30, f32[128,256,128]{1,0,2:T(8,128)} %copy.29, f32[128,256]{1,0:T(8,128)S(1)} %get-tuple-element.50), kind=kOutput, calls=%fused_computation.57 | convolution fusion | flops 562036736 | bytes 42074112 | tf_op jit(solution)/shard_map/hxk,hyk->hyx/dot_general | solution.py:108
  367.9 10.9 %fusion.14 = f32[128,256]{0,1:T(8,128)S(1)} fusion(f32[128,256]{0,1:T(8,128)S(1)} %broadcast_multiply_fusion.6, bf16[64,256,128]{2,0,1:T(8,128)(2,1)} %get-tuple-element.40, bf16[64,256,128]{2,0,1:T(8,128)(2,1)} %get-tuple-element.39), kind=kLoop, calls=%fused_computation.22 | loop fusion | flops 29327360 | bytes 8650752 | tf_op jit(solution)/shard_map/reduce_sum | solution.py:12
  378.9 12.8 %fusion.39 = f32[128,256,128]{2,0,1:T(8,128)} fusion(f32[128,256]{0,1:T(8,128)S(1)} %add_rsqrt_fusion.2, f32[128,256]{0,1:T(8,128)S(1)} %broadcast_multiply_fusion.6, f32[128]{0:T(128)S(1)} %copy-done.34, bf16[128,128]{1,0:T(8,128)(2,1)S(1)} %copy-done, bf16[64,256,128]{2,0,1:T(8,128)(2,1)S(1)} %copy-done.14, bf16[64,256,128]{2,0,1:T(8,128)(2,1)S(1)} %copy-done.13), kind=kOutput, calls=%fused_computation.69 | convolution fusion | flops 1107296256 | bytes 25461248 | tf_op jit(solution)/shard_map/xkd,dh->hxk/dot_general | solution.py:81
  391.7 12.8 %fusion.37 = f32[128,256,128]{2,0,1:T(8,128)} fusion(f32[128,256]{0,1:T(8,128)S(1)} %add_rsqrt_fusion.2, f32[128,256]{0,1:T(8,128)S(1)} %broadcast_multiply_fusion.6, f32[128]{0:T(128)S(1)} %copy-done.34, bf16[128,128]{1,0:T(8,128)(2,1)S(1)} %copy-done.37, bf16[64,256,128]{2,0,1:T(8,128)(2,1)S(1)} %copy-done.14, bf16[64,256,128]{2,0,1:T(8,128)(2,1)S(1)} %copy-done.13), kind=kOutput, calls=%fused_computation.68 | convolution fusion | flops 1107296256 | bytes 25461248 | tf_op jit(solution)/shard_map/xkd,dh->hxk/dot_general | solution.py:80
  410.6 17.7 %copy.31 = f32[128,256,128]{1,0,2:T(8,128)} copy(f32[128,256,128]{2,0,1:T(8,128)} %fusion.39) | data formatting | bytes 33554432 | tf_op jit(solution)/shard_map/xkd,dh->hxk/dot_general | solution.py:81
  428.3 17.8 %copy.32 = f32[128,256,128]{1,0,2:T(8,128)} copy(f32[128,256,128]{2,0,1:T(8,128)} %fusion.37) | data formatting | bytes 33554432 | tf_op jit(solution)/shard_map/xkd,dh->hxk/dot_general | solution.py:80
  452.5 16.9 %fusion.29 = f32[128,64,128]{2,1,0:T(8,128)} fusion(bf16[128,64,256]{2,1,0:T(8,128)(2,1)} %copy.15, f32[128,256,128]{1,0,2:T(8,128)} %copy.32, f32[128,256,128]{1,0,2:T(8,128)} %copy.31, f32[128,256]{1,0:T(8,128)S(1)} %get-tuple-element.48), kind=kOutput, calls=%fused_computation.55 | convolution fusion | flops 562036736 | bytes 42074112 | tf_op jit(solution)/shard_map/hxk,hyk->hyx/dot_general | solution.py:108
  469.4 11.0 %select_convert_fusion.1 = bf16[128,64,128]{2,0,1:T(8,128)(2,1)} fusion(f32[128,64,128]{2,1,0:T(8,128)} %fusion.29, f32[128,64,128]{2,1,0:T(8,128)S(1)} %copy-done.19, pred[]{:T(512)S(6)} %eq.11), kind=kLoop, calls=%fused_computation.97 | loop fusion | flops 1048576 | bytes 10485761 | tf_op jit(solution)/shard_map/convert_element_type | solution.py:128
  495.6 11.1 %fusion.11 = f32[128,256]{0,1:T(8,128)S(1)} fusion(f32[128,256]{0,1:T(8,128)S(1)} %broadcast_multiply_fusion.5, bf16[64,256,128]{2,0,1:T(8,128)(2,1)} %get-tuple-element.34, bf16[64,256,128]{2,0,1:T(8,128)(2,1)} %get-tuple-element.33), kind=kLoop, calls=%fused_computation.19 | loop fusion | flops 29327360 | bytes 8650752 | tf_op jit(solution)/shard_map/reduce_sum | solution.py:12
  506.8 12.8 %fusion.43 = f32[128,256,128]{2,0,1:T(8,128)} fusion(f32[128,256]{0,1:T(8,128)S(1)} %add_rsqrt_fusion.1, f32[128,256]{0,1:T(8,128)S(1)} %broadcast_multiply_fusion.5, f32[128]{0:T(128)S(1)} %copy-done.34, bf16[128,128]{1,0:T(8,128)(2,1)S(1)} %copy-done, bf16[64,256,128]{2,0,1:T(8,128)(2,1)S(1)} %copy-done.10, bf16[64,256,128]{2,0,1:T(8,128)(2,1)S(1)} %copy-done.7), kind=kOutput, calls=%fused_computation.71 | convolution fusion | flops 1107296256 | bytes 25461248 | tf_op jit(solution)/shard_map/xkd,dh->hxk/dot_general | solution.py:81
  519.6 17.8 %copy.34 = f32[128,256,128]{1,0,2:T(8,128)} copy(f32[128,256,128]{2,0,1:T(8,128)} %fusion.43) | data formatting | bytes 33554432 | tf_op jit(solution)/shard_map/xkd,dh->hxk/dot_general | solution.py:81
  537.4 15.0 %fusion.41 = f32[128,256,128]{2,0,1:T(8,128)} fusion(f32[128,256]{0,1:T(8,128)S(1)} %add_rsqrt_fusion.1, f32[128,256]{0,1:T(8,128)S(1)} %broadcast_multiply_fusion.5, f32[128]{0:T(128)S(1)} %copy-done.34, bf16[128,128]{1,0:T(8,128)(2,1)S(1)} %copy-done.37, bf16[64,256,128]{2,0,1:T(8,128)(2,1)} %get-tuple-element.34, bf16[64,256,128]{2,0,1:T(8,128)(2,1)} %get-tuple-element.33), kind=kOutput, calls=%fused_computation.70 | convolution fusion | flops 1107296256 | bytes 25461248 | tf_op jit(solution)/shard_map/xkd,dh->hxk/dot_general | solution.py:80
  552.3 17.8 %copy.35 = f32[128,256,128]{1,0,2:T(8,128)} copy(f32[128,256,128]{2,0,1:T(8,128)} %fusion.41) | data formatting | bytes 33554432 | tf_op jit(solution)/shard_map/xkd,dh->hxk/dot_general | solution.py:80
  595.0 16.5 %fusion.27 = f32[128,64,128]{2,1,0:T(8,128)} fusion(bf16[128,64,256]{2,1,0:T(8,128)(2,1)} %copy.15, f32[128,256,128]{1,0,2:T(8,128)} %copy.35, f32[128,256,128]{1,0,2:T(8,128)} %copy.34, f32[128,256]{1,0:T(8,128)S(1)} %copy-done.32), kind=kOutput, calls=%fused_computation.53 | convolution fusion | flops 562036736 | bytes 42074112 | tf_op jit(solution)/shard_map/hxk,hyk->hyx/dot_general | solution.py:108
  626.8 10.9 %fusion.8 = f32[128,256]{0,1:T(8,128)S(1)} fusion(f32[128,256]{0,1:T(8,128)S(1)} %broadcast_multiply_fusion.4, bf16[64,256,128]{2,0,1:T(8,128)(2,1)} %get-tuple-element.36, bf16[64,256,128]{2,0,1:T(8,128)(2,1)} %get-tuple-element.35), kind=kLoop, calls=%fused_computation.16 | loop fusion | flops 29327360 | bytes 8650752 | tf_op jit(solution)/shard_map/reduce_sum | solution.py:12
  637.7 12.8 %fusion.47 = f32[128,256,128]{2,0,1:T(8,128)} fusion(f32[128,256]{0,1:T(8,128)S(1)} %add_rsqrt_fusion, f32[128,256]{0,1:T(8,128)S(1)} %broadcast_multiply_fusion.4, f32[128]{0:T(128)S(1)} %copy-done.34, bf16[128,128]{1,0:T(8,128)(2,1)S(1)} %copy-done, bf16[64,256,128]{2,0,1:T(8,128)(2,1)S(1)} %copy-done.17, bf16[64,256,128]{2,0,1:T(8,128)(2,1)S(1)} %copy-done.15), kind=kOutput, calls=%fused_computation.73 | convolution fusion | flops 1107296256 | bytes 25461248 | tf_op jit(solution)/shard_map/xkd,dh->hxk/dot_general | solution.py:81
  650.6 12.8 %fusion.45 = f32[128,256,128]{2,0,1:T(8,128)} fusion(f32[128,256]{0,1:T(8,128)S(1)} %add_rsqrt_fusion, f32[128,256]{0,1:T(8,128)S(1)} %broadcast_multiply_fusion.4, f32[128]{0:T(128)S(1)} %copy-done.34, bf16[128,128]{1,0:T(8,128)(2,1)S(1)} %copy-done.37, bf16[64,256,128]{2,0,1:T(8,128)(2,1)S(1)} %copy-done.17, bf16[64,256,128]{2,0,1:T(8,128)(2,1)S(1)} %copy-done.15), kind=kOutput, calls=%fused_computation.72 | convolution fusion | flops 1107296256 | bytes 25461248 | tf_op jit(solution)/shard_map/xkd,dh->hxk/dot_general | solution.py:80
  665.9 17.8 %copy.36 = f32[128,256,128]{1,0,2:T(8,128)} copy(f32[128,256,128]{2,0,1:T(8,128)} %fusion.47) | data formatting | bytes 33554432 | tf_op jit(solution)/shard_map/xkd,dh->hxk/dot_general | solution.py:81
  683.6 17.8 %copy.37 = f32[128,256,128]{1,0,2:T(8,128)} copy(f32[128,256,128]{2,0,1:T(8,128)} %fusion.45) | data formatting | bytes 33554432 | tf_op jit(solution)/shard_map/xkd,dh->hxk/dot_general | solution.py:80
  701.4 16.7 %fusion.25 = f32[128,64,128]{2,1,0:T(8,128)} fusion(bf16[128,64,256]{2,1,0:T(8,128)(2,1)} %copy.15, f32[128,256,128]{1,0,2:T(8,128)} %copy.37, f32[128,256,128]{1,0,2:T(8,128)} %copy.36, f32[128,256]{1,0:T(8,128)S(1)} %copy-done.31), kind=kOutput, calls=%fused_computation.51 | convolution fusion | flops 562036736 | bytes 42074112 | tf_op jit(solution)/shard_map/hxk,hyk->hyx/dot_general | solution.py:108
  718.0 12.4 %select_convert_fusion = bf16[128,64,128]{2,0,1:T(8,128)(2,1)} fusion(f32[128,64,128]{2,1,0:T(8,128)} %fusion.25, f32[128,64,128]{2,1,0:T(8,128)} %fusion.27, pred[]{:T(512)S(6)} %eq.13), kind=kLoop, calls=%fused_computation.93 | loop fusion | flops 1048576 | bytes 10485761 | tf_op jit(solution)/shard_map/convert_element_type | solution.py:128
  (179 shorter events, 154.8 us)
Async XLA Ops:
  0.0 265.6 %copy-start = (bf16[128,128]{1,0:T(8,128)(2,1)S(1)}, bf16[128,128]{1,0:T(8,128)(2,1)}, u32[]{:S(2)}) copy-start(bf16[128,128]{1,0:T(8,128)(2,1)} %param.14) | copy-start | bytes 98308
  5.4 138.7 %collective-permute-start.2 = (bf16[32,256,128]{2,0,1:T(8,128)(2,1)}, bf16[32,256,128]{2,0,1:T(8,128)(2,1)}, u32[]{:S(2)}, u32[]{:S(2)}) collective-permute-start(bf16[32,256,128]{2,0,1:T(8,128)(2,1)} %copy.49), channel_id=1, source_target_pairs={{0,8},{2,10},{4,12},{6,14},{8,0},{10,2},{12,4},{14,6},{1,9},{3,11}... | collective-permute-start | bytes 6291464 | tf_op jit(solution)/shard_map/ppermute | solution.py:49
  8.6 135.6 %collective-permute-start = (bf16[32,256,128]{2,0,1:T(8,128)(2,1)}, bf16[32,256,128]{2,0,1:T(8,128)(2,1)S(1)}, u32[]{:S(2)}, u32[]{:S(2)}) collective-permute-start(bf16[32,256,128]{2,0,1:T(8,128)(2,1)} %copy.49), channel_id=1, source_target_pairs={{0,2},{2,0},{4,6},{6,4},{8,10},{10,8},{12,14},{14,12},{1,3},{3,1},... | collective-permute-start | bytes 6291464 | tf_op jit(solution)/shard_map/ppermute | solution.py:54
  12.5 221.5 %collective-permute-start.3 = (bf16[32,256,128]{2,0,1:T(8,128)(2,1)}, bf16[32,256,128]{2,0,1:T(8,128)(2,1)}, u32[]{:S(2)}, u32[]{:S(2)}) collective-permute-start(bf16[32,256,128]{2,0,1:T(8,128)(2,1)} %copy.50), channel_id=1, source_target_pairs={{0,8},{2,10},{4,12},{6,14},{8,0},{10,2},{12,4},{14,6},{1,9},{3,11}... | collective-permute-start | bytes 6291464 | tf_op jit(solution)/shard_map/ppermute | solution.py:49
  12.6 221.5 %collective-permute-start.1 = (bf16[32,256,128]{2,0,1:T(8,128)(2,1)}, bf16[32,256,128]{2,0,1:T(8,128)(2,1)}, u32[]{:S(2)}, u32[]{:S(2)}) collective-permute-start(bf16[32,256,128]{2,0,1:T(8,128)(2,1)} %copy.50), channel_id=1, source_target_pairs={{0,2},{2,0},{4,6},{6,4},{8,10},{10,8},{12,14},{14,12},{1,3},{3,1},... | collective-permute-start | bytes 6291464 | tf_op jit(solution)/shard_map/ppermute | solution.py:54
  50.1 187.6 %copy-start.2 = (bf16[64,256,128]{2,1,0:T(8,128)(2,1)S(1)}, bf16[64,256,128]{2,1,0:T(8,128)(2,1)}, u32[]{:S(2)}) copy-start(bf16[64,256,128]{2,1,0:T(8,128)(2,1)} %param.10) | copy-start | bytes 12582916
  144.1 206.2 %collective-permute-start.4 = (bf16[32,256,128]{2,0,1:T(8,128)(2,1)}, bf16[32,256,128]{2,0,1:T(8,128)(2,1)}, u32[]{:S(2)}, u32[]{:S(2)}) collective-permute-start(bf16[32,256,128]{2,0,1:T(8,128)(2,1)} %collective-permute-done.2), channel_id=1, source_target_pairs={{0,2},{2,0},{4,6},{6,4},{8,10},{10,8},{12,14},{14,12},{1,3},{3,1},... | collective-permute-start | bytes 6291464 | tf_op jit(solution)/shard_map/ppermute | solution.py:54
  145.1 205.2 %collective-permute-start.8 = (bf16[32,256,128]{2,0,1:T(8,128)(2,1)}, bf16[32,256,128]{2,0,1:T(8,128)(2,1)}, u32[]{:S(2)}, u32[]{:S(2)}) collective-permute-start(bf16[32,256,128]{2,0,1:T(8,128)(2,1)} %copy.49), channel_id=1, source_target_pairs={{0,4},{2,6},{4,8},{6,10},{8,12},{10,14},{12,0},{14,2},{1,5},{3,7},... | collective-permute-start | bytes 6291464 | tf_op jit(solution)/shard_map/ppermute | solution.py:49
  234.0 122.3 %collective-permute-start.5 = (bf16[32,256,128]{2,0,1:T(8,128)(2,1)}, bf16[32,256,128]{2,0,1:T(8,128)(2,1)}, u32[]{:S(2)}, u32[]{:S(2)}) collective-permute-start(bf16[32,256,128]{2,0,1:T(8,128)(2,1)} %collective-permute-done.3), channel_id=1, source_target_pairs={{0,2},{2,0},{4,6},{6,4},{8,10},{10,8},{12,14},{14,12},{1,3},{3,1},... | collective-permute-start | bytes 6291464 | tf_op jit(solution)/shard_map/ppermute | solution.py:54
  235.0 169.5 %collective-permute-start.9 = (bf16[32,256,128]{2,0,1:T(8,128)(2,1)}, bf16[32,256,128]{2,0,1:T(8,128)(2,1)}, u32[]{:S(2)}, u32[]{:S(2)}) collective-permute-start(bf16[32,256,128]{2,0,1:T(8,128)(2,1)} %copy.50), channel_id=1, source_target_pairs={{0,4},{2,6},{4,8},{6,10},{8,12},{10,14},{12,0},{14,2},{1,5},{3,7},... | collective-permute-start | bytes 6291464 | tf_op jit(solution)/shard_map/ppermute | solution.py:49
  254.6 11.1 %copy-start.3 = (bf16[64,256,128]{2,0,1:T(8,128)(2,1)S(1)}, bf16[64,256,128]{2,0,1:T(8,128)(2,1)}, u32[]{:S(2)}) copy-start(bf16[64,256,128]{2,0,1:T(8,128)(2,1)} %get-tuple-element.37) | copy-start | bytes 12582916
  278.5 17.8 %copy-start.37 = (bf16[128,128]{1,0:T(8,128)(2,1)S(1)}, bf16[128,128]{1,0:T(8,128)(2,1)}, u32[]{:S(2)}) copy-start(bf16[128,128]{1,0:T(8,128)(2,1)} %param.13) | copy-start | bytes 98308
  350.3 130.1 %collective-permute-start.10 = (bf16[32,256,128]{2,0,1:T(8,128)(2,1)}, bf16[32,256,128]{2,0,1:T(8,128)(2,1)}, u32[]{:S(2)}, u32[]{:S(2)}) collective-permute-start(bf16[32,256,128]{2,0,1:T(8,128)(2,1)} %collective-permute-done.8), channel_id=1, source_target_pairs={{0,2},{2,0},{4,6},{6,4},{8,10},{10,8},{12,14},{14,12},{1,3},{3,1},... | collective-permute-start | bytes 6291464 | tf_op jit(solution)/shard_map/ppermute | solution.py:54
  350.8 129.6 %collective-permute-start.12 = (bf16[32,256,128]{2,0,1:T(8,128)(2,1)}, bf16[32,256,128]{2,0,1:T(8,128)(2,1)}, u32[]{:S(2)}, u32[]{:S(2)}) collective-permute-start(bf16[32,256,128]{2,0,1:T(8,128)(2,1)} %copy.49), channel_id=1, source_target_pairs={{0,12},{2,14},{4,0},{6,2},{8,4},{10,6},{12,8},{14,10},{1,13},{3,15... | collective-permute-start | bytes 6291464 | tf_op jit(solution)/shard_map/ppermute | solution.py:49
  391.7 13.8 %copy-start.4 = (bf16[64,256,128]{2,0,1:T(8,128)(2,1)S(1)}, bf16[64,256,128]{2,0,1:T(8,128)(2,1)}, u32[]{:S(2)}) copy-start(bf16[64,256,128]{2,0,1:T(8,128)(2,1)} %get-tuple-element.37) | copy-start | bytes 12582916
  391.7 13.8 %copy-start.6 = (bf16[64,256,128]{2,0,1:T(8,128)(2,1)S(1)}, bf16[64,256,128]{2,0,1:T(8,128)(2,1)}, u32[]{:S(2)}) copy-start(bf16[64,256,128]{2,0,1:T(8,128)(2,1)} %get-tuple-element.38) | copy-start | bytes 12582916
  404.5 76.2 %collective-permute-start.11 = (bf16[32,256,128]{2,0,1:T(8,128)(2,1)}, bf16[32,256,128]{2,0,1:T(8,128)(2,1)}, u32[]{:S(2)}, u32[]{:S(2)}) collective-permute-start(bf16[32,256,128]{2,0,1:T(8,128)(2,1)} %collective-permute-done.9), channel_id=1, source_target_pairs={{0,2},{2,0},{4,6},{6,4},{8,10},{10,8},{12,14},{14,12},{1,3},{3,1},... | collective-permute-start | bytes 6291464 | tf_op jit(solution)/shard_map/ppermute | solution.py:54
  405.5 75.2 %collective-permute-start.13 = (bf16[32,256,128]{2,0,1:T(8,128)(2,1)}, bf16[32,256,128]{2,0,1:T(8,128)(2,1)}, u32[]{:S(2)}, u32[]{:S(2)}) collective-permute-start(bf16[32,256,128]{2,0,1:T(8,128)(2,1)} %copy.50), channel_id=1, source_target_pairs={{0,12},{2,14},{4,0},{6,2},{8,4},{10,6},{12,8},{14,10},{1,13},{3,15... | collective-permute-start | bytes 6291464 | tf_op jit(solution)/shard_map/ppermute | solution.py:49
  407.7 162.4 %collective-permute-start.6 = (bf16[128,64,128]{2,0,1:T(8,128)(2,1)}, bf16[128,64,128]{2,0,1:T(8,128)(2,1)}, u32[]{:S(2)}, u32[]{:S(2)}) collective-permute-start(bf16[128,64,128]{2,0,1:T(8,128)(2,1)} %broadcast_select_fusion.9), channel_id=1, source_target_pairs={{0,1},{1,0},{2,3},{3,2},{4,5},{5,4},{6,7},{7,6},{8,9},{9,8},{10,11... | collective-permute-start | bytes 6291464 | tf_op jit(solution)/shard_map/ppermute | solution.py:57
  452.5 16.9 %copy-start.19 = (f32[128,64,128]{2,1,0:T(8,128)S(1)}, f32[128,64,128]{2,1,0:T(8,128)}, u32[]{:S(2)}) copy-start(f32[128,64,128]{2,1,0:T(8,128)} %fusion.31) | copy-start | bytes 12582916
  480.4 95.6 %collective-permute-start.7 = (bf16[128,64,128]{2,0,1:T(8,128)(2,1)}, bf16[128,64,128]{2,0,1:T(8,128)(2,1)}, u32[]{:S(2)}, u32[]{:S(2)}) collective-permute-start(bf16[128,64,128]{2,0,1:T(8,128)(2,1)} %select_convert_fusion.1), channel_id=1, source_target_pairs={{0,1},{1,0},{2,3},{3,2},{4,5},{5,4},{6,7},{7,6},{8,9},{9,8},{10,11... | collective-permute-start | bytes 6291464 | tf_op jit(solution)/shard_map/ppermute | solution.py:57
  480.4 131.1 %collective-permute-start.14 = (bf16[32,256,128]{2,0,1:T(8,128)(2,1)}, bf16[32,256,128]{2,0,1:T(8,128)(2,1)}, u32[]{:S(2)}, u32[]{:S(2)}) collective-permute-start(bf16[32,256,128]{2,0,1:T(8,128)(2,1)} %collective-permute-done.12), channel_id=1, source_target_pairs={{0,2},{2,0},{4,6},{6,4},{8,10},{10,8},{12,14},{14,12},{1,3},{3,1},... | collective-permute-start | bytes 6291464 | tf_op jit(solution)/shard_map/ppermute | solution.py:54
  480.7 133.1 %collective-permute-start.15 = (bf16[32,256,128]{2,0,1:T(8,128)(2,1)}, bf16[32,256,128]{2,0,1:T(8,128)(2,1)}, u32[]{:S(2)}, u32[]{:S(2)}) collective-permute-start(bf16[32,256,128]{2,0,1:T(8,128)(2,1)} %collective-permute-done.13), channel_id=1, source_target_pairs={{0,2},{2,0},{4,6},{6,4},{8,10},{10,8},{12,14},{14,12},{1,3},{3,1},... | collective-permute-start | bytes 6291464 | tf_op jit(solution)/shard_map/ppermute | solution.py:54
  495.6 11.2 %copy-start.7 = (bf16[64,256,128]{2,0,1:T(8,128)(2,1)S(1)}, bf16[64,256,128]{2,0,1:T(8,128)(2,1)}, u32[]{:S(2)}) copy-start(bf16[64,256,128]{2,0,1:T(8,128)(2,1)} %get-tuple-element.33) | copy-start | bytes 12582916
  495.6 11.2 %copy-start.10 = (bf16[64,256,128]{2,0,1:T(8,128)(2,1)S(1)}, bf16[64,256,128]{2,0,1:T(8,128)(2,1)}, u32[]{:S(2)}) copy-start(bf16[64,256,128]{2,0,1:T(8,128)(2,1)} %get-tuple-element.34) | copy-start | bytes 12582916
  650.6 12.8 %copy-start.8 = (bf16[64,256,128]{2,0,1:T(8,128)(2,1)S(1)}, bf16[64,256,128]{2,0,1:T(8,128)(2,1)}, u32[]{:S(2)}) copy-start(bf16[64,256,128]{2,0,1:T(8,128)(2,1)} %get-tuple-element.33) | copy-start | bytes 12582916
  650.6 12.8 %copy-start.11 = (bf16[64,256,128]{2,0,1:T(8,128)(2,1)S(1)}, bf16[64,256,128]{2,0,1:T(8,128)(2,1)}, u32[]{:S(2)}) copy-start(bf16[64,256,128]{2,0,1:T(8,128)(2,1)} %get-tuple-element.34) | copy-start | bytes 12582916
  665.5 69.6 %collective-permute-start.16 = (bf16[128,64,128]{2,0,1:T(8,128)(2,1)}, bf16[128,64,128]{2,0,1:T(8,128)(2,1)}, u32[]{:S(2)}, u32[]{:S(2)}) collective-permute-start(bf16[128,64,128]{2,0,1:T(8,128)(2,1)} %broadcast_select_fusion.8), channel_id=1, source_target_pairs={{0,1},{1,0},{2,3},{3,2},{4,5},{5,4},{6,7},{7,6},{8,9},{9,8},{10,11... | collective-permute-start | bytes 6291464 | tf_op jit(solution)/shard_map/ppermute | solution.py:57
  683.6 17.8 %copy-start.31 = (f32[128,256]{1,0:T(8,128)S(1)}, f32[128,256]{1,0:T(8,128)}, u32[]{:S(2)}) copy-start(f32[128,256]{1,0:T(8,128)} %get-tuple-element.49) | copy-start | bytes 393220
  718.0 13.6 %copy-start.28 = (f32[128,64,128]{2,0,1:T(8,128)S(1)}, f32[128,64,128]{2,0,1:T(8,128)}, u32[]{:S(2)}) copy-start(f32[128,64,128]{2,0,1:T(8,128)} %fusion.67) | copy-start | bytes 12582916
  718.0 13.6 %copy-start.38 = (bf16[128,128]{1,0:T(8,128)(2,1)S(1)}, bf16[128,128]{1,0:T(8,128)(2,1)}, u32[]{:S(2)}) copy-start(bf16[128,128]{1,0:T(8,128)(2,1)} %param.19) | copy-start | bytes 98308
  730.5 17.0 %collective-permute-start.17 = (bf16[128,64,128]{2,0,1:T(8,128)(2,1)}, bf16[128,64,128]{2,0,1:T(8,128)(2,1)}, u32[]{:S(2)}, u32[]{:S(2)}) collective-permute-start(bf16[128,64,128]{2,0,1:T(8,128)(2,1)} %select_convert_fusion), channel_id=1, source_target_pairs={{0,1},{1,0},{2,3},{3,2},{4,5},{5,4},{6,7},{7,6},{8,9},{9,8},{10,11... | collective-permute-start | bytes 6291464 | tf_op jit(solution)/shard_map/ppermute | solution.py:57
  (26 other events, 169.4 us)

commit v2 on v1

--- a/solution.py
+++ b/solution.py
@@ -1,9 +1,95 @@
+import functools
+
 import jax
 import jax.numpy as jnp
 from jax import lax
+from jax.experimental import pallas as pl
+from jax.experimental.pallas import tpu as pltpu
 from jax.sharding import PartitionSpec as P
 
 CHUNKS = 2
+STEP = 16
+
+
+def left_kernel(parts, steps, place_ref, *refs):
+    blocks = refs[:parts]
+    mask_ref, gain_ref, weight_ref, right_ref, out_ref, active, slab, left = refs[parts:]
+    at = pl.program_id(0)
+    for part in range(parts):
+
+        @pl.when(at // steps == part)
+        def _():
+            active[...] = blocks[part][...]
+
+    hidden = weight_ref.shape[0] // 2
+    gain = gain_ref[...]
+    base = pl.multiple_of(lax.rem(at * STEP + place_ref[0], left.shape[1]), STEP)
+
+    def row(x, carry):
+        normed = norm_last(active[x].astype(jnp.float32), gain).astype(jnp.bfloat16)
+        both = lax.dot_general(
+            weight_ref[...], normed, (((1,), (1,)), ((), ())), preferred_element_type=jnp.float32
+        )
+        gate = 0.5 * jnp.tanh(0.5 * both[hidden:]) + 0.5
+        slab[x] = gate * (both[:hidden] * mask_ref[pl.ds(base + x, 1), :])
+        return carry
+
+    lax.fori_loop(0, STEP, row, None, unroll=4)
+    for c in range(0, hidden, 16):
+        left[c : c + 16, pl.ds(base, STEP), :] = jnp.swapaxes(slab[:, c : c + 16, :], 0, 1).astype(
+            jnp.bfloat16
+        )
+
+    @pl.when(at == parts * steps - 1)
+    def _():
+        def head(h, carry):
+            out_ref[h] = lax.dot_general(
+                right_ref[h], left[h], (((1,), (1,)), ((), ())), preferred_element_type=jnp.float32
+            )
+            return carry
+
+        lax.fori_loop(0, hidden, head, None, unroll=4)
+
+
+def left_product(blocks, place, mask, gain, weight, right):
+    parts = len(blocks)
+    rows, depth, channels = blocks[0].shape
+    steps = rows // STEP
+    hidden, wide, _ = right.shape
+    width = parts * rows
+
+    def part_spec(part):
+        return pl.BlockSpec(
+            (STEP, depth, channels), lambda g, p: (jnp.clip(g - part * steps, 0, steps - 1), 0, 0)
+        )
+
+    def whole(a):
+        return pl.BlockSpec(a.shape, lambda g, p: (0,) * a.ndim)
+
+    return pl.pallas_call(
+        functools.partial(left_kernel, parts, steps),
+        grid_spec=pltpu.PrefetchScalarGridSpec(
+            num_scalar_prefetch=1,
+            grid=(parts * steps,),
+            in_specs=[part_spec(i) for i in range(parts)]
+            + [whole(mask), whole(gain), whole(weight), whole(right)],
+            out_specs=pl.BlockSpec((hidden, wide, width), lambda g, p: (0, 0, 0)),
+            scratch_shapes=[
+                pltpu.VMEM((STEP, depth, channels), jnp.bfloat16),
+                pltpu.VMEM((STEP, hidden, depth), jnp.float32),
+                pltpu.VMEM((hidden, width, depth), jnp.bfloat16),
+            ],
+        ),
+        out_shape=jax.ShapeDtypeStruct((hidden, wide, width), jnp.float32),
+        compiler_params=pltpu.CompilerParams(
+            vmem_limit_bytes=50 * 2**20, dimension_semantics=("arbitrary",)
+        ),
+        cost_estimate=pl.CostEstimate(
+            flops=2 * width * depth * (channels * 2 * hidden + hidden * wide),
+            bytes_accessed=20 * 2**20,
+            transcendentals=width * depth * hidden,
+        ),
+    )(place, *blocks, mask, gain, weight, right)
 
 
 def norm_last(values, gains):
@@ -90,32 +176,43 @@
     )
     width = 2 * rows_tile
 
-    def block_of(d):
-        held = jnp.concatenate([mine[d, n] for n in range(CHUNKS)], axis=0)
-        swapped = jnp.concatenate([other[d, n] for n in range(CHUNKS)], axis=0)
+    left_weight = jnp.concatenate([left_proj, left_gate], axis=1).T
+    place = (side_at * rows_tile).astype(jnp.int32)[None]
+
+    def source_pair(d):
+        return lax.rem(pair_at - d + n_pairs, n_pairs)
+
+    def product(d):
+        rows_mask = lax.dynamic_slice_in_dim(mask_values, source_pair(d) * width, width)
+        blocks = [mine[d, n] for n in range(CHUNKS)] + [other[d, n] for n in range(CHUNKS)]
+        return left_product(
+            blocks,
+            place,
+            rows_mask[:, None] * mask_cols[None, :],
+            in_gain[None],
+            left_weight,
+            right_side,
+        )
+
+    column_at = lax.rem(row_at * rows_tile, cols_tile)
+    column_core = (row_at * rows_tile) // cols_tile
+
+    def columns_of(d):
+        def cut(chunks):
+            return jnp.concatenate(
+                [lax.dynamic_slice_in_dim(c, column_at, rows_tile, 1) for c in chunks], axis=0
+            )
+
+        held = cut([mine[d, n] for n in range(CHUNKS)])
+        swapped = cut([other[d, n] for n in range(CHUNKS)])
         first = jnp.where(side_at == 0, held, swapped)
         second = jnp.where(side_at == 0, swapped, held)
         return jnp.concatenate([first, second], axis=0)
 
-    def source_pair(d):
-        return lax.rem(pair_at - d + n_pairs, n_pairs)
-
-    def product(block, d):
-        rows_mask = lax.dynamic_slice_in_dim(mask_values, source_pair(d) * width, width)
-        left_side = gated(
-            normalise(block), left_proj, left_gate, rows_mask[:, None] * mask_cols[None, :]
-        )
-        return jnp.einsum("hxk,hyk->hyx", left_side, right_side, preferred_element_type=jnp.float32)
-
-    column_at = lax.rem(row_at * rows_tile, cols_tile)
-    column_core = (row_at * rows_tile) // cols_tile
-
     out = jnp.zeros((rows_tile, cols_tile, channels), jnp.bfloat16)
     for d in range(half_pairs):
-        near, far = block_of(d), block_of(d + half_pairs)
         keep_near = source_pair(d) // half_pairs == col_at
-        near_pair = lax.dynamic_slice_in_dim(near, column_at, rows_tile, 1)
-        far_pair = lax.dynamic_slice_in_dim(far, column_at, rows_tile, 1)
+        near_pair, far_pair = columns_of(d), columns_of(d + half_pairs)
         kept_pair = jnp.where(keep_near, near_pair, far_pair)
         got_pair = sibling(jnp.where(keep_near, far_pair, near_pair))
         turned = jnp.where(column_core == col_at, kept_pair, got_pair)
@@ -124,7 +221,7 @@
                 "ijd,dc->jic", normalise(turned), out_gate, preferred_element_type=jnp.float32
             )
         )
-        near_sum, far_sum = product(near, d), product(far, d + half_pairs)
+        near_sum, far_sum = product(d), product(d + half_pairs)
         got_sum = sibling(jnp.where(keep_near, far_sum, near_sum).astype(jnp.bfloat16))
         combined = jnp.where(keep_near, near_sum, far_sum) + got_sum.astype(jnp.float32)
         combined_norm = norm_first(combined, out_gain).astype(jnp.bfloat16)
@@ -133,8 +230,8 @@
         )
         swapped = jnp.transpose(turned, (1, 0, 2)).astype(jnp.float32)
         result = (swapped + gate_values * update).astype(jnp.bfloat16)
-        place = lax.rem(pair_at - d + n_pairs, half_pairs)
-        out = lax.dynamic_update_slice(out, result, (0, place * width, 0))
+        spot = lax.rem(pair_at - d + n_pairs, half_pairs)
+        out = lax.dynamic_update_slice(out, result, (0, spot * width, 0))
     return out
 
 

time: 769 us -> 598 us (0.78)
  matrix products: 206 us -> 33.1 us
  Pallas kernels: 0 us -> 146 us
  local copies, waits for them, and re-layouts: 197 us -> 53.7 us
  other arithmetic: 154 us -> 48.3 us
  waiting for transfers between devices: 182 us -> 284 us
    pallas_call x0 -> x4, Pallas kernels: none -> 146 us  [left_product(): pl.pallas_call(functools.partial(left_kernel, parts, steps), grid_spec=pl...]
    ppermute x8, waiting for transfers between devices: 0.02 us -> 100 us  [across(): return lax.ppermute(block, 'rows', [(r, r ^ 1) for r in range(n_rows)])]
    dot_general x4 -> x0, matrix products: 67.1 us -> none  [product(): jnp.einsum('hxk,hyk->hyx', left_side, right_side, preferred_element_type=...]
    dot_general x4 -> x1, local copies, waits for them, and re-layouts: 71 us -> 9.19 us  [gated(): jnp.einsum('xkd,dh->hxk', normed, w_gate, preferred_element_type=jnp.floa...]
    dot_general x4 -> x1, local copies, waits for them, and re-layouts: 71 us -> 9.21 us  [gated(): jnp.einsum('xkd,dh->hxk', normed, w_proj, preferred_element_type=jnp.floa...]
    dot_general x5 -> x1, matrix products: 67.4 us -> 8.5 us  [gated(): jnp.einsum('xkd,dh->hxk', normed, w_proj, preferred_element_type=jnp.floa...]
    dot_general x5 -> x1, matrix products: 59.1 us -> 8.53 us  [gated(): jnp.einsum('xkd,dh->hxk', normed, w_gate, preferred_element_type=jnp.floa...]
    reduce_sum x7 -> x3, other arithmetic: 55.1 us -> 10.2 us  [norm_last(): spread = jnp.mean(centred * centred, axis=-1, keepdims=True)]
  transfers between devices with their start and end apart: 18 -> 18, of which waited for: 2 -> 7; matrix products, arithmetic and copies ran while one was open for 64% -> 16% of each run, Pallas kernels for 0% -> 25%
where the time goes in v2:
time: 598 us; the launch traced here: 589 us
  waiting for transfers between devices  284 us (47%)
  Pallas kernels  146 us (24%)
  local copies, waits for them, and re-layouts  53.7 us (9%)
  other arithmetic  48.3 us (8%)
  matrix products  33.1 us (6%)
  starting transfers between devices  22.3 us (4%)
    ppermute x6, waiting for transfers between devices, along(): lax.ppermute(block, 'rows', [(r, (r + 2 * step) % n_rows) for r in range(...  184 us
    pallas_call x4, Pallas kernels, left_product(): pl.pallas_call(functools.partial(left_kernel, parts, steps), grid_spec=pl...  146 us
    ppermute x8, waiting for transfers between devices, across(): return lax.ppermute(block, 'rows', [(r, r ^ 1) for r in range(n_rows)])  100 us
    dynamic_slice x15, local copies, waits for them, and re-layouts, cut(): lax.dynamic_slice_in_dim(c, column_at, rows_tile, 1)  12.4 us
  transfers between devices with their start and end apart: 18, of which 7 were waited for; matrix products, arithmetic and copies ran while one was open for 16% of the time, Pallas kernels for 25%

profile of v2, /device:TPU:1, one launch (start us, length us, event | category | flops | bytes accessed | tf_op | source)
XLA Modules:
  0.0 589.2 jit_solution(6403796506609348202)
XLA Ops:
  0.0 4.2 fusion.42
  4.3 3.1 collective-permute-start.3
  10.1 4.8 fusion.2
  15.2 8.5 %fusion.22 = f32[64,256,128]{2,1,0:T(8,128)} fusion(bf16[64,256,128]{2,1,0:T(8,128)(2,1)} %param.10, f32[128]{0:T(128)S(1)} %copy-done.2, f32[64,256]{1,0:T(8,128)S(1)} %add_rsqrt_fusion.1, f32[64,256]{1,0:T(8,128)S(1)} %broadcast_multiply_fusion.5, bf16[128,128]{1,0:T(8,128)(2,1)S(1)} %copy-done), kind=kOutput, calls=%fused_computation.40 | convolution fusion | flops 547356672 | bytes 12747264 | tf_op jit(solution)/shard_map/xkd,dh->hxk/dot_general | solution.py:167
  23.7 9.2 %copy.15 = f32[64,256,128]{1,0,2:T(8,128)} copy(f32[64,256,128]{2,1,0:T(8,128)} %fusion.22) | data formatting | bytes 16777216 | tf_op jit(solution)/shard_map/xkd,dh->hxk/dot_general | solution.py:167
  32.9 8.5 %fusion.20 = f32[64,256,128]{2,1,0:T(8,128)} fusion(bf16[64,256,128]{2,1,0:T(8,128)(2,1)} %param.10, f32[128]{0:T(128)S(1)} %copy-done.2, f32[64,256]{1,0:T(8,128)S(1)} %add_rsqrt_fusion.1, f32[64,256]{1,0:T(8,128)S(1)} %broadcast_multiply_fusion.5, bf16[128,128]{1,0:T(8,128)(2,1)S(1)} %copy-done.24), kind=kOutput, calls=%fused_computation.39 | convolution fusion | flops 547356672 | bytes 12747264 | tf_op jit(solution)/shard_map/xkd,dh->hxk/dot_general | solution.py:166
  41.4 9.2 %copy.16 = f32[64,256,128]{1,0,2:T(8,128)} copy(f32[64,256,128]{2,1,0:T(8,128)} %fusion.20) | data formatting | bytes 16777216 | tf_op jit(solution)/shard_map/xkd,dh->hxk/dot_general | solution.py:166
  52.2 90.7 %collective-permute-done.3.refs_1_ = bf16[32,256,128]{2,1,0:T(8,128)(2,1)} collective-permute-done((bf16[32,256,128]{2,1,0:T(8,128)(2,1)}, bf16[32,256,128]{2,1,0:T(8,128)(2,1)}, u32[]{:S(2)}, u32[]{:S(2)}) %collective-permute-start.3) | collective-permute-done | bytes 2097184 | tf_op jit(solution)/shard_map/ppermute | solution.py:135
  145.4 87.4 %collective-permute-done.2.refs_0_ = bf16[32,256,128]{2,1,0:T(8,128)(2,1)} collective-permute-done((bf16[32,256,128]{2,1,0:T(8,128)(2,1)S(1)}, bf16[32,256,128]{2,1,0:T(8,128)(2,1)}, u32[]{:S(2)}, u32[]{:S(2)}) %collective-permute-start.2) | collective-permute-done | bytes 2097184 | tf_op jit(solution)/shard_map/ppermute | solution.py:135
  233.8 8.7 %fusion.19.refs_7_ = bf16[128,64,256]{2,1,0:T(8,128)(2,1)} fusion(f32[64,256]{1,0:T(8,128)S(1)} %broadcast_multiply_fusion.4, f32[64,256,128]{1,0,2:T(8,128)} %copy.16, f32[64,256,128]{1,0,2:T(8,128)} %copy.15), kind=kLoop, calls=%fused_computation.38 | loop fusion | flops 12582912 | bytes 21037056 | tf_op jit(solution)/shard_map/convert_element_type | solution.py:168
  247.8 3.3 collective-permute-start.13
  251.1 27.8 %collective-permute-done.4.refs_2_ = bf16[32,256,128]{2,1,0:T(8,128)(2,1)S(1)} collective-permute-done((bf16[32,256,128]{2,1,0:T(8,128)(2,1)}, bf16[32,256,128]{2,1,0:T(8,128)(2,1)S(1)}, u32[]{:S(2)}, u32[]{:S(2)}) %collective-permute-start.4) | collective-permute-done | bytes 2097184 | tf_op jit(solution)/shard_map/ppermute | solution.py:140
  288.9 36.5 %shard_map.100 = f32[128,64,128]{2,1,0:T(8,128)} custom-call(s32[1]{0:T(128)} %bitcast.3.place_ref, bf16[32,256,128]{2,1,0:T(8,128)(2,1)S(1)} %get-tuple-element.21.refs_0_, bf16[32,256,128]{2,1,0:T(8,128)(2,1)} %get-tuple-element.22.refs_1_, bf16[32,256,128]{2,1,0:T(8,128)(2,1)} %collective-permute-done.refs_2_, ...), custom_call_target="tpu_custom_call" | custom-call | flops 2684354560 | bytes 20971520 | tf_op jit(solution)/shard_map/pallas_call | solution.py:69
  325.4 36.9 %shard_map.101 = f32[128,64,128]{2,1,0:T(8,128)} custom-call(s32[1]{0:T(128)} %bitcast.3.place_ref, bf16[32,256,128]{2,1,0:T(8,128)(2,1)} %collective-permute-done.2.refs_0_, bf16[32,256,128]{2,1,0:T(8,128)(2,1)} %collective-permute-done.3.refs_1_, bf16[32,256,128]{2,1,0:T(8,128)(2,1)} %copy-done.21, bf16[32,256,128]{2,1,0:T(8,128)(2,1)} %copy-done.20, ...), custom_call_target="tpu_custom_call" | custom-call | flops 2684354560 | bytes 20971520 | tf_op jit(solution)/shard_map/pallas_call | solution.py:69
  369.4 3.8 collective-permute-done.12.refs_0_
  377.3 3.7 convert_reduce_fusion.2
  381.0 2.7 fusion.12
  383.8 3.3 fusion.41
  387.0 28.7 %collective-permute-done.15.refs_3_ = bf16[32,256,128]{2,1,0:T(8,128)(2,1)} collective-permute-done((bf16[32,256,128]{2,1,0:T(8,128)(2,1)}, bf16[32,256,128]{2,1,0:T(8,128)(2,1)}, u32[]{:S(2)}, u32[]{:S(2)}) %collective-permute-start.15) | collective-permute-done | bytes 2097184 | tf_op jit(solution)/shard_map/ppermute | solution.py:140
  416.8 43.9 %collective-permute-done.14.refs_2_ = bf16[32,256,128]{2,1,0:T(8,128)(2,1)} collective-permute-done((bf16[32,256,128]{2,1,0:T(8,128)(2,1)S(1)}, bf16[32,256,128]{2,1,0:T(8,128)(2,1)}, u32[]{:S(2)}, u32[]{:S(2)}) %collective-permute-start.14) | collective-permute-done | bytes 2097184 | tf_op jit(solution)/shard_map/ppermute | solution.py:140
  465.5 36.3 %shard_map.102 = f32[128,64,128]{2,1,0:T(8,128)} custom-call(s32[1]{0:T(128)} %bitcast.3.place_ref, bf16[32,256,128]{2,1,0:T(8,128)(2,1)S(1)} %collective-permute-done.8.refs_0_, bf16[32,256,128]{2,1,0:T(8,128)(2,1)} %collective-permute-done.9.refs_1_, bf16[32,256,128]{2,1,0:T(8,128)(2,1)} %collective-permute-done.10.refs_2_, ...), custom_call_target="tpu_custom_call" | custom-call | flops 2684354560 | bytes 20971520 | tf_op jit(solution)/shard_map/pallas_call | solution.py:69
  502.3 36.5 %shard_map.103 = f32[128,64,128]{2,1,0:T(8,128)} custom-call(s32[1]{0:T(128)} %bitcast.3.place_ref, bf16[32,256,128]{2,1,0:T(8,128)(2,1)S(1)} %collective-permute-done.12.refs_0_, bf16[32,256,128]{2,1,0:T(8,128)(2,1)} %collective-permute-done.13.refs_1_, bf16[32,256,128]{2,1,0:T(8,128)(2,1)} %collective-permute-done.14.refs_2_, ...), custom_call_target="tpu_custom_call" | custom-call | flops 2684354560 | bytes 20971520 | tf_op jit(solution)/shard_map/pallas_call | solution.py:69
  538.8 3.2 select_convert_fusion
  542.2 4.8 fusion.24
  547.0 3.5 convert_reduce_fusion.1
  550.6 2.7 fusion.9
  553.4 5.0 fusion.26
  558.3 3.3 fusion.40
  562.3 3.2 multiply_convert_fusion.1
  565.5 4.6 copy.31
  570.1 4.8 copy.27
  574.9 4.9 fusion.18
  (136 shorter events, 50.3 us)
Async XLA Ops:
  0.0 15.2 %copy-start = (bf16[128,128]{1,0:T(8,128)(2,1)S(1)}, bf16[128,128]{1,0:T(8,128)(2,1)}, u32[]{:S(2)}) copy-start(bf16[128,128]{1,0:T(8,128)(2,1)} %param.16) | copy-start | bytes 98308
  0.0 8.9 %copy-start.3 = (bf16[64,256,128]{2,1,0:T(8,128)(2,1)S(1)}, bf16[64,256,128]{2,1,0:T(8,128)(2,1)}, u32[]{:S(2)}) copy-start(bf16[64,256,128]{2,1,0:T(8,128)(2,1)} %param.10) | copy-start | bytes 12582916
  4.3 138.7 %collective-permute-start.3 = (bf16[32,256,128]{2,1,0:T(8,128)(2,1)}, bf16[32,256,128]{2,1,0:T(8,128)(2,1)}, u32[]{:S(2)}, u32[]{:S(2)}) collective-permute-start(bf16[32,256,128]{2,1,0:T(8,128)(2,1)} %get-tuple-element.22.refs_1_), channel_id=1, source_target_pairs={{0,8},{2,10},{4,12},{6,14},{8,0},{10,2},{12,4},{14,6},{1,9},{3,11}... | collective-permute-start | bytes 6291464 | tf_op jit(solution)/shard_map/ppermute | solution.py:135
  7.4 135.6 %collective-permute-start.1 = (bf16[32,256,128]{2,1,0:T(8,128)(2,1)}, bf16[32,256,128]{2,1,0:T(8,128)(2,1)}, u32[]{:S(2)}, u32[]{:S(2)}) collective-permute-start(bf16[32,256,128]{2,1,0:T(8,128)(2,1)} %get-tuple-element.22.refs_1_), channel_id=1, source_target_pairs={{0,2},{2,0},{4,6},{6,4},{8,10},{10,8},{12,14},{14,12},{1,3},{3,1},... | collective-permute-start | bytes 6291464 | tf_op jit(solution)/shard_map/ppermute | solution.py:140
  8.6 224.2 %collective-permute-start.2 = (bf16[32,256,128]{2,1,0:T(8,128)(2,1)S(1)}, bf16[32,256,128]{2,1,0:T(8,128)(2,1)}, u32[]{:S(2)}, u32[]{:S(2)}) collective-permute-start(bf16[32,256,128]{2,1,0:T(8,128)(2,1)S(1)} %get-tuple-element.21.refs_0_), channel_id=1, source_target_pairs={{0,8},{2,10},{4,12},{6,14},{8,0},{10,2},{12,4},{14,6},{1,9},{3,11}... | collective-permute-start | bytes 6291464 | tf_op jit(solution)/shard_map/ppermute | solution.py:135
  8.7 224.1 %collective-permute-start = (bf16[32,256,128]{2,1,0:T(8,128)(2,1)S(1)}, bf16[32,256,128]{2,1,0:T(8,128)(2,1)}, u32[]{:S(2)}, u32[]{:S(2)}) collective-permute-start(bf16[32,256,128]{2,1,0:T(8,128)(2,1)S(1)} %get-tuple-element.21.refs_0_), channel_id=1, source_target_pairs={{0,2},{2,0},{4,6},{6,4},{8,10},{10,8},{12,14},{14,12},{1,3},{3,1},... | collective-permute-start | bytes 6291464 | tf_op jit(solution)/shard_map/ppermute | solution.py:140
  23.7 9.2 %copy-start.24 = (bf16[128,128]{1,0:T(8,128)(2,1)S(1)}, bf16[128,128]{1,0:T(8,128)(2,1)}, u32[]{:S(2)}) copy-start(bf16[128,128]{1,0:T(8,128)(2,1)} %param.15) | copy-start | bytes 98308
  41.4 9.2 %copy-start.25 = (bf16[128,128]{1,0:T(8,128)(2,1)S(1)}, bf16[128,128]{1,0:T(8,128)(2,1)}, u32[]{:S(2)}) copy-start(bf16[128,128]{1,0:T(8,128)(2,1)} %param.13) | copy-start | bytes 98308
  41.4 9.3 %copy-start.26 = (bf16[128,128]{1,0:T(8,128)(2,1)S(1)}, bf16[128,128]{1,0:T(8,128)(2,1)}, u32[]{:S(2)}) copy-start(bf16[128,128]{1,0:T(8,128)(2,1)} %param.14) | copy-start | bytes 98308
  142.9 102.8 %collective-permute-start.5 = (bf16[32,256,128]{2,1,0:T(8,128)(2,1)}, bf16[32,256,128]{2,1,0:T(8,128)(2,1)S(1)}, u32[]{:S(2)}, u32[]{:S(2)}) collective-permute-start(bf16[32,256,128]{2,1,0:T(8,128)(2,1)} %collective-permute-done.3.refs_1_), channel_id=1, source_target_pairs={{0,2},{2,0},{4,6},{6,4},{8,10},{10,8},{12,14},{14,12},{1,3},{3,1},... | collective-permute-start | bytes 6291464 | tf_op jit(solution)/shard_map/ppermute | solution.py:140
  143.9 101.9 %collective-permute-start.9 = (bf16[32,256,128]{2,1,0:T(8,128)(2,1)}, bf16[32,256,128]{2,1,0:T(8,128)(2,1)}, u32[]{:S(2)}, u32[]{:S(2)}) collective-permute-start(bf16[32,256,128]{2,1,0:T(8,128)(2,1)} %get-tuple-element.22.refs_1_), channel_id=1, source_target_pairs={{0,4},{2,6},{4,8},{6,10},{8,12},{10,14},{12,0},{14,2},{1,5},{3,7},... | collective-permute-start | bytes 6291464 | tf_op jit(solution)/shard_map/ppermute | solution.py:135
  232.8 46.1 %collective-permute-start.4 = (bf16[32,256,128]{2,1,0:T(8,128)(2,1)}, bf16[32,256,128]{2,1,0:T(8,128)(2,1)S(1)}, u32[]{:S(2)}, u32[]{:S(2)}) collective-permute-start(bf16[32,256,128]{2,1,0:T(8,128)(2,1)} %collective-permute-done.2.refs_0_), channel_id=1, source_target_pairs={{0,2},{2,0},{4,6},{6,4},{8,10},{10,8},{12,14},{14,12},{1,3},{3,1},... | collective-permute-start | bytes 6291464 | tf_op jit(solution)/shard_map/ppermute | solution.py:140
  233.8 47.2 %collective-permute-start.8 = (bf16[32,256,128]{2,1,0:T(8,128)(2,1)S(1)}, bf16[32,256,128]{2,1,0:T(8,128)(2,1)S(1)}, u32[]{:S(2)}, u32[]{:S(2)}) collective-permute-start(bf16[32,256,128]{2,1,0:T(8,128)(2,1)S(1)} %get-tuple-element.21.refs_0_), channel_id=1, source_target_pairs={{0,4},{2,6},{4,8},{6,10},{8,12},{10,14},{12,0},{14,2},{1,5},{3,7},... | collective-permute-start | bytes 6291464 | tf_op jit(solution)/shard_map/ppermute | solution.py:135
  245.8 38.2 %copy-start.20 = (bf16[32,256,128]{2,1,0:T(8,128)(2,1)}, bf16[32,256,128]{2,1,0:T(8,128)(2,1)S(1)}, u32[]{:S(2)}) copy-start(bf16[32,256,128]{2,1,0:T(8,128)(2,1)S(1)} %collective-permute-done.5.refs_3_) | copy-start | bytes 6291460
  245.8 118.9 %collective-permute-start.11 = (bf16[32,256,128]{2,1,0:T(8,128)(2,1)}, bf16[32,256,128]{2,1,0:T(8,128)(2,1)}, u32[]{:S(2)}, u32[]{:S(2)}) collective-permute-start(bf16[32,256,128]{2,1,0:T(8,128)(2,1)} %collective-permute-done.9.refs_1_), channel_id=1, source_target_pairs={{0,2},{2,0},{4,6},{6,4},{8,10},{10,8},{12,14},{14,12},{1,3},{3,1},... | collective-permute-start | bytes 6291464 | tf_op jit(solution)/shard_map/ppermute | solution.py:140
  247.8 38.4 %copy-start.10 = (bf16[64,64,128]{2,1,0:T(8,128)(2,1)}, bf16[64,64,128]{2,1,0:T(8,128)(2,1)S(1)}, u32[]{:S(2)}) copy-start(bf16[64,64,128]{2,1,0:T(8,128)(2,1)S(1)} %get-tuple-element.40) | copy-start | bytes 3145732
  247.8 120.3 %collective-permute-start.13 = (bf16[32,256,128]{2,1,0:T(8,128)(2,1)}, bf16[32,256,128]{2,1,0:T(8,128)(2,1)}, u32[]{:S(2)}, u32[]{:S(2)}) collective-permute-start(bf16[32,256,128]{2,1,0:T(8,128)(2,1)} %get-tuple-element.22.refs_1_), channel_id=1, source_target_pairs={{0,12},{2,14},{4,0},{6,2},{8,4},{10,6},{12,8},{14,10},{1,13},{3,15... | collective-permute-start | bytes 6291464 | tf_op jit(solution)/shard_map/ppermute | solution.py:135
  281.0 88.4 %collective-permute-start.10 = (bf16[32,256,128]{2,1,0:T(8,128)(2,1)S(1)}, bf16[32,256,128]{2,1,0:T(8,128)(2,1)}, u32[]{:S(2)}, u32[]{:S(2)}) collective-permute-start(bf16[32,256,128]{2,1,0:T(8,128)(2,1)S(1)} %collective-permute-done.8.refs_0_), channel_id=1, source_target_pairs={{0,2},{2,0},{4,6},{6,4},{8,10},{10,8},{12,14},{14,12},{1,3},{3,1},... | collective-permute-start | bytes 6291464 | tf_op jit(solution)/shard_map/ppermute | solution.py:140
  281.8 91.5 %collective-permute-start.12 = (bf16[32,256,128]{2,1,0:T(8,128)(2,1)S(1)}, bf16[32,256,128]{2,1,0:T(8,128)(2,1)S(1)}, u32[]{:S(2)}, u32[]{:S(2)}) collective-permute-start(bf16[32,256,128]{2,1,0:T(8,128)(2,1)S(1)} %get-tuple-element.21.refs_0_), channel_id=1, source_target_pairs={{0,12},{2,14},{4,0},{6,2},{8,4},{10,6},{12,8},{14,10},{1,13},{3,15... | collective-permute-start | bytes 6291464 | tf_op jit(solution)/shard_map/ppermute | solution.py:135
  284.2 41.2 %copy-start.12 = (bf16[64,64,128]{2,1,0:T(8,128)(2,1)}, bf16[64,64,128]{2,1,0:T(8,128)(2,1)S(1)}, u32[]{:S(2)}) copy-start(bf16[64,64,128]{2,1,0:T(8,128)(2,1)S(1)} %get-tuple-element.41) | copy-start | bytes 3145732
  284.2 41.2 %copy-start.14 = (bf16[64,64,128]{2,1,0:T(8,128)(2,1)}, bf16[64,64,128]{2,1,0:T(8,128)(2,1)S(1)}, u32[]{:S(2)}) copy-start(bf16[64,64,128]{2,1,0:T(8,128)(2,1)S(1)} %get-tuple-element.42) | copy-start | bytes 3145732
  286.2 91.1 %collective-permute-start.6 = (bf16[128,64,128]{2,1,0:T(8,128)(2,1)}, bf16[128,64,128]{2,1,0:T(8,128)(2,1)}, u32[]{:S(2)}, u32[]{:S(2)}) collective-permute-start(bf16[128,64,128]{2,1,0:T(8,128)(2,1)} %broadcast_select_fusion.1), channel_id=1, source_target_pairs={{0,1},{1,0},{2,3},{3,2},{4,5},{5,4},{6,7},{7,6},{8,9},{9,8},{10,11... | collective-permute-start | bytes 6291464 | tf_op jit(solution)/shard_map/ppermute | solution.py:143
  325.4 36.9 %copy-start.4 = (f32[128,64,128]{2,1,0:T(8,128)S(1)}, f32[128,64,128]{2,1,0:T(8,128)}, u32[]{:S(2)}) copy-start(f32[128,64,128]{2,1,0:T(8,128)} %shard_map.100) | copy-start | bytes 12582916
  364.7 19.0 %collective-permute-start.7 = (bf16[128,64,128]{2,1,0:T(8,128)(2,1)}, bf16[128,64,128]{2,1,0:T(8,128)(2,1)}, u32[]{:S(2)}, u32[]{:S(2)}) collective-permute-start(bf16[128,64,128]{2,1,0:T(8,128)(2,1)} %select_convert_fusion.1), channel_id=1, source_target_pairs={{0,1},{1,0},{2,3},{3,2},{4,5},{5,4},{6,7},{7,6},{8,9},{9,8},{10,11... | collective-permute-start | bytes 6291464 | tf_op jit(solution)/shard_map/ppermute | solution.py:143
  368.1 9.2 %copy-start.11 = (bf16[64,64,128]{2,1,0:T(8,128)(2,1)S(1)}, bf16[64,64,128]{2,1,0:T(8,128)(2,1)}, u32[]{:S(2)}) copy-start(bf16[64,64,128]{2,1,0:T(8,128)(2,1)} %copy-done.10) | copy-start | bytes 3145732
  368.1 9.2 %copy-start.13 = (bf16[64,64,128]{2,1,0:T(8,128)(2,1)S(1)}, bf16[64,64,128]{2,1,0:T(8,128)(2,1)}, u32[]{:S(2)}) copy-start(bf16[64,64,128]{2,1,0:T(8,128)(2,1)} %copy-done.12) | copy-start | bytes 3145732
  368.1 9.2 %copy-start.15 = (bf16[64,64,128]{2,1,0:T(8,128)(2,1)S(1)}, bf16[64,64,128]{2,1,0:T(8,128)(2,1)}, u32[]{:S(2)}) copy-start(bf16[64,64,128]{2,1,0:T(8,128)(2,1)} %copy-done.14) | copy-start | bytes 3145732
  368.1 47.6 %collective-permute-start.15 = (bf16[32,256,128]{2,1,0:T(8,128)(2,1)}, bf16[32,256,128]{2,1,0:T(8,128)(2,1)}, u32[]{:S(2)}, u32[]{:S(2)}) collective-permute-start(bf16[32,256,128]{2,1,0:T(8,128)(2,1)} %collective-permute-done.13.refs_1_), channel_id=1, source_target_pairs={{0,2},{2,0},{4,6},{6,4},{8,10},{10,8},{12,14},{14,12},{1,3},{3,1},... | collective-permute-start | bytes 6291464 | tf_op jit(solution)/shard_map/ppermute | solution.py:140
  373.2 87.4 %collective-permute-start.14 = (bf16[32,256,128]{2,1,0:T(8,128)(2,1)S(1)}, bf16[32,256,128]{2,1,0:T(8,128)(2,1)}, u32[]{:S(2)}, u32[]{:S(2)}) collective-permute-start(bf16[32,256,128]{2,1,0:T(8,128)(2,1)S(1)} %collective-permute-done.12.refs_0_), channel_id=1, source_target_pairs={{0,2},{2,0},{4,6},{6,4},{8,10},{10,8},{12,14},{14,12},{1,3},{3,1},... | collective-permute-start | bytes 6291464 | tf_op jit(solution)/shard_map/ppermute | solution.py:140
  464.7 82.3 %collective-permute-start.16 = (bf16[128,64,128]{2,1,0:T(8,128)(2,1)}, bf16[128,64,128]{2,1,0:T(8,128)(2,1)}, u32[]{:S(2)}, u32[]{:S(2)}) collective-permute-start(bf16[128,64,128]{2,1,0:T(8,128)(2,1)} %broadcast_select_fusion), channel_id=1, source_target_pairs={{0,1},{1,0},{2,3},{3,2},{4,5},{5,4},{6,7},{7,6},{8,9},{9,8},{10,11... | collective-permute-start | bytes 6291464 | tf_op jit(solution)/shard_map/ppermute | solution.py:143
  542.1 16.2 %collective-permute-start.17 = (bf16[128,64,128]{2,1,0:T(8,128)(2,1)S(1)}, bf16[128,64,128]{2,1,0:T(8,128)(2,1)}, u32[]{:S(2)}, u32[]{:S(2)}) collective-permute-start(bf16[128,64,128]{2,1,0:T(8,128)(2,1)S(1)} %select_convert_fusion), channel_id=1, source_target_pairs={{0,1},{1,0},{2,3},{3,2},{4,5},{5,4},{6,7},{7,6},{8,9},{9,8},{10,11... | collective-permute-start | bytes 6291464 | tf_op jit(solution)/shard_map/ppermute | solution.py:143
  565.5 9.4 %copy-start.29 = (bf16[128,128]{1,0:T(8,128)(2,1)S(1)}, bf16[128,128]{1,0:T(8,128)(2,1)}, u32[]{:S(2)}) copy-start(bf16[128,128]{1,0:T(8,128)(2,1)} %param.19) | copy-start | bytes 98308
  (16 other events, 85.9 us)

commit v3 on v2

--- a/solution.py
+++ b/solution.py
@@ -85,7 +85,7 @@
             vmem_limit_bytes=50 * 2**20, dimension_semantics=("arbitrary",)
         ),
         cost_estimate=pl.CostEstimate(
-            flops=2 * width * depth * (channels * 2 * hidden + hidden * wide),
+            flops=32 * width * depth * (channels * 2 * hidden + hidden * wide),
             bytes_accessed=20 * 2**20,
             transcendentals=width * depth * hidden,
         ),
@@ -142,25 +142,13 @@
     def sibling(block):
         return lax.ppermute(block, "cols", [(0, 1), (1, 0)])
 
-    def after(value, *others):
-        return lax.optimization_barrier((value, *others))[0]
-
-    order = [d + h * half_pairs for d in range(half_pairs) for h in (0, 1)]
     chunk_rows = rows_tile // CHUNKS
     own = [pair[n * chunk_rows : (n + 1) * chunk_rows] for n in range(CHUNKS)]
     mine, other = {}, {}
-    z_queue, y_queue = [], []
-    for d in order:
+    for d in range(n_pairs):
         for n in range(CHUNKS):
-            if d == 0:
-                mine[d, n] = own[n]
-            else:
-                source = own[n] if len(z_queue) < 2 else after(own[n], z_queue[-2])
-                mine[d, n] = along(source, d)
-                z_queue.append(mine[d, n])
-            source = mine[d, n] if len(y_queue) < 2 else after(mine[d, n], y_queue[-2])
-            other[d, n] = across(source)
-            y_queue.append(other[d, n])
+            mine[d, n] = own[n] if d == 0 else along(mine[d - 1, n], 1)
+            other[d, n] = across(mine[d, n])
 
     def gated(normed, w_proj, w_gate, pair_mask):
         projected = jnp.einsum("xkd,dh->hxk", normed, w_proj, preferred_element_type=jnp.float32)
@@ -209,6 +197,7 @@
         second = jnp.where(side_at == 0, swapped, held)
         return jnp.concatenate([first, second], axis=0)
 
+    products = [product(d) for d in range(n_pairs)]
     out = jnp.zeros((rows_tile, cols_tile, channels), jnp.bfloat16)
     for d in range(half_pairs):
         keep_near = source_pair(d) // half_pairs == col_at
@@ -221,7 +210,7 @@
                 "ijd,dc->jic", normalise(turned), out_gate, preferred_element_type=jnp.float32
             )
         )
-        near_sum, far_sum = product(d), product(d + half_pairs)
+        near_sum, far_sum = products[d], products[d + half_pairs]
         got_sum = sibling(jnp.where(keep_near, far_sum, near_sum).astype(jnp.bfloat16))
         combined = jnp.where(keep_near, near_sum, far_sum) + got_sum.astype(jnp.float32)
         combined_norm = norm_first(combined, out_gain).astype(jnp.bfloat16)

time: 598 us -> 479 us (0.80); the launches traced: 589 us -> 477 us
  waiting for transfers between devices: 284 us -> 169 us
    ppermute x8, waiting for transfers between devices: 100 us -> 35.6 us  [across(): return lax.ppermute(block, 'rows', [(r, r ^ 1) for r in range(n_rows)])]
    ppermute x6, waiting for transfers between devices: 184 us -> 134 us  [along(): lax.ppermute(block, 'rows', [(r, (r + 2 * step) % n_rows) for r in range(...]
  transfers between devices with their start and end apart: 18 -> 18, of which waited for: 7 -> 4; matrix products, arithmetic and copies ran while one was open for 16% -> 22% of each run, Pallas kernels for 25% -> 31%
where the time goes in v3:
time: 479 us; the launch traced here: 477 us
  waiting for transfers between devices  169 us (35%)
  Pallas kernels  146 us (30%)
  local copies, waits for them, and re-layouts  55.2 us (12%)
  other arithmetic  54.1 us (11%)
  matrix products  32.5 us (7%)
  starting transfers between devices  19.6 us (4%)
    pallas_call x4, Pallas kernels, left_product(): pl.pallas_call(functools.partial(left_kernel, parts, steps), grid_spec=pl...  146 us
    ppermute x6, waiting for transfers between devices, along(): lax.ppermute(block, 'rows', [(r, (r + 2 * step) % n_rows) for r in range(...  134 us
    ppermute x8, waiting for transfers between devices, across(): return lax.ppermute(block, 'rows', [(r, r ^ 1) for r in range(n_rows)])  35.6 us
    dynamic_slice x15, local copies, waits for them, and re-layouts, cut(): lax.dynamic_slice_in_dim(c, column_at, rows_tile, 1)  14.1 us
    reduce_sum x3, other arithmetic, norm_last(): spread = jnp.mean(centred * centred, axis=-1, keepdims=True)  11.5 us
    reduce_sum x3, other arithmetic, norm_last(): average = jnp.mean(values, axis=-1, keepdims=True)  10.6 us
    ppermute x4, starting transfers between devices, sibling(): return lax.ppermute(block, 'cols', [(0, 1), (1, 0)])  9.86 us
    dot_general x2, matrix products, body(): jnp.einsum('ijd,dc->jic', normalise(turned), out_gate, preferred_element_...  9.82 us
  transfers between devices with their start and end apart: 18, of which 4 were waited for; matrix products, arithmetic and copies ran while one was open for 22% of the time, Pallas kernels for 31%

profile of v3, /device:TPU:1, one launch (start us, length us, event | category | flops | bytes accessed | tf_op | source)
XLA Modules:
  0.0 477.4 jit_solution(14214279797462581645)
XLA Ops:
  0.0 4.0 fusion.42
  8.9 3.4 convert_reduce_fusion
  12.6 6.1 %fusion.2 = f32[64,256]{1,0:T(8,128)S(1)} fusion(bf16[64,256,128]{2,1,0:T(8,128)(2,1)} %param.10, f32[64,256]{1,0:T(8,128)S(1)} %broadcast_multiply_fusion.5), kind=kLoop, calls=%fused_computation.4 | loop fusion | flops 8372224 | bytes 4325376 | tf_op jit(solution)/shard_map/reduce_sum | solution.py:98
  18.8 7.8 %fusion.22 = f32[64,256,128]{2,1,0:T(8,128)} fusion(bf16[64,256,128]{2,1,0:T(8,128)(2,1)S(1)} %copy-done.3, f32[128]{0:T(128)S(1)} %copy-done.2, f32[64,256]{1,0:T(8,128)S(1)} %add_rsqrt_fusion.1, f32[64,256]{1,0:T(8,128)S(1)} %broadcast_multiply_fusion.5, bf16[128,128]{1,0:T(8,128)(2,1)S(1)} %copy-done), kind=kOutput, calls=%fused_computation.40 | convolution fusion | flops 547356672 | bytes 12747264 | tf_op jit(solution)/shard_map/xkd,dh->hxk/dot_general | solution.py:155
  26.6 9.3 %copy.15 = f32[64,256,128]{1,0,2:T(8,128)} copy(f32[64,256,128]{2,1,0:T(8,128)} %fusion.22) | data formatting | bytes 16777216 | tf_op jit(solution)/shard_map/xkd,dh->hxk/dot_general | solution.py:155
  35.9 8.6 %fusion.20 = f32[64,256,128]{2,1,0:T(8,128)} fusion(bf16[64,256,128]{2,1,0:T(8,128)(2,1)} %param.10, f32[128]{0:T(128)S(1)} %copy-done.2, f32[64,256]{1,0:T(8,128)S(1)} %add_rsqrt_fusion.1, f32[64,256]{1,0:T(8,128)S(1)} %broadcast_multiply_fusion.5, bf16[128,128]{1,0:T(8,128)(2,1)S(1)} %copy-done.25), kind=kOutput, calls=%fused_computation.39 | convolution fusion | flops 547356672 | bytes 12747264 | tf_op jit(solution)/shard_map/xkd,dh->hxk/dot_general | solution.py:154
  44.5 9.3 %copy.16 = f32[64,256,128]{1,0,2:T(8,128)} copy(f32[64,256,128]{2,1,0:T(8,128)} %fusion.20) | data formatting | bytes 16777216 | tf_op jit(solution)/shard_map/xkd,dh->hxk/dot_general | solution.py:154
  55.5 8.7 %fusion.19.refs_7_ = bf16[128,64,256]{2,1,0:T(8,128)(2,1)} fusion(f32[64,256]{1,0:T(8,128)S(1)} %broadcast_multiply_fusion.4, f32[64,256,128]{1,0,2:T(8,128)} %copy.16, f32[64,256,128]{1,0,2:T(8,128)} %copy.15), kind=kLoop, calls=%fused_computation.38 | loop fusion | flops 12582912 | bytes 21037056 | tf_op jit(solution)/shard_map/convert_element_type | solution.py:156
  64.2 34.3 %collective-permute-done.4.refs_1_ = bf16[32,256,128]{2,1,0:T(8,128)(2,1)} collective-permute-done((bf16[32,256,128]{2,1,0:T(8,128)(2,1)}, bf16[32,256,128]{2,1,0:T(8,128)(2,1)}, u32[]{:S(2)}, u32[]{:S(2)}) %collective-permute-start.4) | collective-permute-done | bytes 2097184 | tf_op jit(solution)/shard_map/ppermute | solution.py:135
  100.5 36.3 %shard_map.100 = f32[128,64,128]{2,1,0:T(8,128)} custom-call(s32[1]{0:T(128)} %bitcast.3.place_ref, bf16[32,256,128]{2,1,0:T(8,128)(2,1)S(1)} %get-tuple-element.13.refs_0_, bf16[32,256,128]{2,1,0:T(8,128)(2,1)} %get-tuple-element.14.refs_1_, bf16[32,256,128]{2,1,0:T(8,128)(2,1)} %collective-permute-done.refs_2_, ...), custom_call_target="tpu_custom_call" | custom-call | flops 42949672960 | bytes 20971520 | tf_op jit(solution)/shard_map/pallas_call | solution.py:69
  141.4 50.1 %collective-permute-done.3.refs_0_ = bf16[32,256,128]{2,1,0:T(8,128)(2,1)S(1)} collective-permute-done((bf16[32,256,128]{2,1,0:T(8,128)(2,1)}, bf16[32,256,128]{2,1,0:T(8,128)(2,1)S(1)}, u32[]{:S(2)}, u32[]{:S(2)}) %collective-permute-start.3) | collective-permute-done | bytes 2097184 | tf_op jit(solution)/shard_map/ppermute | solution.py:135
  197.3 36.7 %shard_map.102 = f32[128,64,128]{2,1,0:T(8,128)} custom-call(s32[1]{0:T(128)} %bitcast.3.place_ref, bf16[32,256,128]{2,1,0:T(8,128)(2,1)} %collective-permute-done.2.refs_0_, bf16[32,256,128]{2,1,0:T(8,128)(2,1)} %collective-permute-done.4.refs_1_, bf16[32,256,128]{2,1,0:T(8,128)(2,1)} %collective-permute-done.10.refs_2_, ...), custom_call_target="tpu_custom_call" | custom-call | flops 42949672960 | bytes 20971520 | tf_op jit(solution)/shard_map/pallas_call | solution.py:69
  233.9 49.3 %collective-permute-done.13.refs_1_ = bf16[32,256,128]{2,1,0:T(8,128)(2,1)} collective-permute-done((bf16[32,256,128]{2,1,0:T(8,128)(2,1)S(1)}, bf16[32,256,128]{2,1,0:T(8,128)(2,1)}, u32[]{:S(2)}, u32[]{:S(2)}) %collective-permute-start.13) | collective-permute-done | bytes 2097184 | tf_op jit(solution)/shard_map/ppermute | solution.py:135
  284.7 36.5 %shard_map.101 = f32[128,64,128]{2,1,0:T(8,128)} custom-call(s32[1]{0:T(128)} %bitcast.3.place_ref, bf16[32,256,128]{2,1,0:T(8,128)(2,1)S(1)} %collective-permute-done.3.refs_0_, bf16[32,256,128]{2,1,0:T(8,128)(2,1)} %copy-done.24, bf16[32,256,128]{2,1,0:T(8,128)(2,1)} %collective-permute-done.6.refs_2_, ...), custom_call_target="tpu_custom_call" | custom-call | flops 42949672960 | bytes 20971520 | tf_op jit(solution)/shard_map/pallas_call | solution.py:69
  323.7 5.9 %collective-permute-start.9 = (bf16[128,64,128]{2,1,0:T(8,128)(2,1)}, bf16[128,64,128]{2,1,0:T(8,128)(2,1)}, u32[]{:S(2)}, u32[]{:S(2)}) collective-permute-start(bf16[128,64,128]{2,1,0:T(8,128)(2,1)} %select_convert_fusion.1), channel_id=1, source_target_pairs={{0,1},{1,0},{2,3},{3,2},{4,5},{5,4},{6,7},{7,6},{8,9},{9,8},{10,11... | collective-permute-start | bytes 6291464 | tf_op jit(solution)/shard_map/ppermute | solution.py:143
  337.0 35.6 %collective-permute-done.14.refs_2_ = bf16[32,256,128]{2,1,0:T(8,128)(2,1)} collective-permute-done((bf16[32,256,128]{2,1,0:T(8,128)(2,1)S(1)}, bf16[32,256,128]{2,1,0:T(8,128)(2,1)}, u32[]{:S(2)}, u32[]{:S(2)}) %collective-permute-start.14) | collective-permute-done | bytes 2097184 | tf_op jit(solution)/shard_map/ppermute | solution.py:140
  375.8 4.0 collective-permute-start.16
  379.8 36.5 %shard_map.103 = f32[128,64,128]{2,1,0:T(8,128)} custom-call(s32[1]{0:T(128)} %bitcast.3.place_ref, bf16[32,256,128]{2,1,0:T(8,128)(2,1)S(1)} %collective-permute-done.12.refs_0_, bf16[32,256,128]{2,1,0:T(8,128)(2,1)} %collective-permute-done.13.refs_1_, bf16[32,256,128]{2,1,0:T(8,128)(2,1)} %collective-permute-done.14.refs_2_, ...), custom_call_target="tpu_custom_call" | custom-call | flops 42949672960 | bytes 20971520 | tf_op jit(solution)/shard_map/pallas_call | solution.py:69
  416.3 4.8 %select_convert_fusion = bf16[128,64,128]{2,1,0:T(8,128)(2,1)} fusion(f32[128,64,128]{2,1,0:T(8,128)} %shard_map.103, f32[128,64,128]{2,1,0:T(8,128)S(1)} %copy-done.5, pred[]{:T(512)S(6)} %eq.13), kind=kLoop, calls=%fused_computation.33 | loop fusion | flops 1048576 | bytes 10485761 | tf_op jit(solution)/shard_map/convert_element_type | solution.py:214
  421.1 3.1 fusion.41
  424.2 3.5 convert_reduce_fusion.2
  427.8 2.7 fusion.12
  431.0 4.8 %fusion.24 = f32[128,64,128]{2,1,0:T(8,128)} fusion(bf16[128,64,128]{2,1,0:T(8,128)(2,1)S(1)} %get-tuple-element.12, f32[128]{0:T(128)S(1)} %copy-done.2, f32[128,64]{1,0:T(8,128)S(1)} %add_rsqrt_fusion.2, f32[128,64]{1,0:T(8,128)S(1)} %broadcast_multiply_fusion.7, bf16[128,128]{1,0:T(8,128)(2,1)S(1)} %copy-done.23), kind=kOutput, calls=%fused_computation.41 | convolution fusion | flops 273678336 | bytes 6390272 | tf_op jit(solution)/shard_map/ijd,dc->jic/dot_general | solution.py:209
  435.9 3.7 convert_reduce_fusion.1
  439.7 2.7 fusion.9
  442.4 5.0 %fusion.26 = f32[128,64,128]{2,1,0:T(8,128)} fusion(bf16[128,64,128]{2,1,0:T(8,128)(2,1)S(1)} %get-tuple-element.8, f32[128,64]{1,0:T(8,128)S(1)} %add_rsqrt_fusion, f32[128,64]{1,0:T(8,128)S(1)} %broadcast_multiply_fusion.6, f32[128]{0:T(128)S(1)} %copy-done.2, bf16[128,128]{1,0:T(8,128)(2,1)S(1)} %copy-done.23), kind=kOutput, calls=%fused_computation.42 | convolution fusion | flops 273678336 | bytes 6390272 | tf_op jit(solution)/shard_map/ijd,dc->jic/dot_general | solution.py:209
  447.4 3.0 fusion.40
  451.0 3.3 multiply_convert_fusion.1
  454.3 4.6 copy.31
  458.9 4.6 copy.27
  463.5 4.9 %fusion.18 = bf16[64,128,128]{2,0,1:T(8,128)(2,1)S(1)} fusion(bf16[128,64,128]{2,1,0:T(8,128)(2,1)} %copy-done.4, f32[128,64,128]{2,1,0:T(8,128)} %fusion.26, bf16[128,64,128]{0,1,2:T(8,128)(2,1)} %copy.31, bf16[128,128]{1,0:T(8,128)(2,1)S(1)} %copy-done.30), kind=kOutput, calls=%fused_computation.27 | convolution fusion | flops 275775488 | bytes 10518528 | tf_op jit(solution)/shard_map/hji,hd->jid/dot_general | solution.py:217
  474.7 2.7 copy_dynamic-update-slice_fusion
  (138 shorter events, 41.1 us)
Async XLA Ops:
  0.0 18.7 %copy-start = (bf16[128,128]{1,0:T(8,128)(2,1)S(1)}, bf16[128,128]{1,0:T(8,128)(2,1)}, u32[]{:S(2)}) copy-start(bf16[128,128]{1,0:T(8,128)(2,1)} %param.16) | copy-start | bytes 98308
  4.0 8.4 %copy-start.28 = (s32[512]{0:T(512)S(1)}, s32[512]{0:T(512)}, u32[]{:S(2)}) copy-start(s32[512]{0:T(512)} %param.11) | copy-start | bytes 6148
  4.0 95.6 %collective-permute-start.2 = (bf16[32,256,128]{2,1,0:T(8,128)(2,1)S(1)}, bf16[32,256,128]{2,1,0:T(8,128)(2,1)}, u32[]{:S(2)}, u32[]{:S(2)}) collective-permute-start(bf16[32,256,128]{2,1,0:T(8,128)(2,1)S(1)} %get-tuple-element.13.refs_0_), channel_id=1, source_target_pairs={{0,4},{2,6},{4,8},{6,10},{8,12},{10,14},{12,0},{14,2},{1,5},{3,7},... | collective-permute-start | bytes 6291464 | tf_op jit(solution)/shard_map/ppermute | solution.py:135
  6.2 94.1 %collective-permute-start = (bf16[32,256,128]{2,1,0:T(8,128)(2,1)S(1)}, bf16[32,256,128]{2,1,0:T(8,128)(2,1)}, u32[]{:S(2)}, u32[]{:S(2)}) collective-permute-start(bf16[32,256,128]{2,1,0:T(8,128)(2,1)S(1)} %get-tuple-element.13.refs_0_), channel_id=1, source_target_pairs={{0,2},{2,0},{4,6},{6,4},{8,10},{10,8},{12,14},{14,12},{1,3},{3,1},... | collective-permute-start | bytes 6291464 | tf_op jit(solution)/shard_map/ppermute | solution.py:140
  7.4 91.2 %collective-permute-start.4 = (bf16[32,256,128]{2,1,0:T(8,128)(2,1)}, bf16[32,256,128]{2,1,0:T(8,128)(2,1)}, u32[]{:S(2)}, u32[]{:S(2)}) collective-permute-start(bf16[32,256,128]{2,1,0:T(8,128)(2,1)} %get-tuple-element.14.refs_1_), channel_id=1, source_target_pairs={{0,4},{2,6},{4,8},{6,10},{8,12},{10,14},{12,0},{14,2},{1,5},{3,7},... | collective-permute-start | bytes 6291464 | tf_op jit(solution)/shard_map/ppermute | solution.py:135
  8.7 91.8 %collective-permute-start.1 = (bf16[32,256,128]{2,1,0:T(8,128)(2,1)}, bf16[32,256,128]{2,1,0:T(8,128)(2,1)}, u32[]{:S(2)}, u32[]{:S(2)}) collective-permute-start(bf16[32,256,128]{2,1,0:T(8,128)(2,1)} %get-tuple-element.14.refs_1_), channel_id=1, source_target_pairs={{0,2},{2,0},{4,6},{6,4},{8,10},{10,8},{12,14},{14,12},{1,3},{3,1},... | collective-permute-start | bytes 6291464 | tf_op jit(solution)/shard_map/ppermute | solution.py:140
  8.9 9.8 %copy-start.2 = (f32[128]{0:T(128)S(1)}, f32[128]{0:T(128)}, u32[]{:S(2)}) copy-start(f32[128]{0:T(128)} %param.12) | copy-start | bytes 1540
  26.6 9.3 %copy-start.25 = (bf16[128,128]{1,0:T(8,128)(2,1)S(1)}, bf16[128,128]{1,0:T(8,128)(2,1)}, u32[]{:S(2)}) copy-start(bf16[128,128]{1,0:T(8,128)(2,1)} %param.15) | copy-start | bytes 98308
  44.5 9.3 %copy-start.26 = (bf16[128,128]{1,0:T(8,128)(2,1)S(1)}, bf16[128,128]{1,0:T(8,128)(2,1)}, u32[]{:S(2)}) copy-start(bf16[128,128]{1,0:T(8,128)(2,1)} %param.13) | copy-start | bytes 98308
  44.5 9.4 %copy-start.27 = (bf16[128,128]{1,0:T(8,128)(2,1)S(1)}, bf16[128,128]{1,0:T(8,128)(2,1)}, u32[]{:S(2)}) copy-start(bf16[128,128]{1,0:T(8,128)(2,1)} %param.14) | copy-start | bytes 98308
  98.6 97.0 %collective-permute-start.5 = (bf16[32,256,128]{2,1,0:T(8,128)(2,1)}, bf16[32,256,128]{2,1,0:T(8,128)(2,1)S(1)}, u32[]{:S(2)}, u32[]{:S(2)}) collective-permute-start(bf16[32,256,128]{2,1,0:T(8,128)(2,1)} %collective-permute-done.4.refs_1_), channel_id=1, source_target_pairs={{0,4},{2,6},{4,8},{6,10},{8,12},{10,14},{12,0},{14,2},{1,5},{3,7},... | collective-permute-start | bytes 6291464 | tf_op jit(solution)/shard_map/ppermute | solution.py:135
  98.6 93.6 %collective-permute-start.11 = (bf16[32,256,128]{2,1,0:T(8,128)(2,1)}, bf16[32,256,128]{2,1,0:T(8,128)(2,1)}, u32[]{:S(2)}, u32[]{:S(2)}) collective-permute-start(bf16[32,256,128]{2,1,0:T(8,128)(2,1)} %collective-permute-done.4.refs_1_), channel_id=1, source_target_pairs={{0,2},{2,0},{4,6},{6,4},{8,10},{10,8},{12,14},{14,12},{1,3},{3,1},... | collective-permute-start | bytes 6291464 | tf_op jit(solution)/shard_map/ppermute | solution.py:140
  99.6 91.8 %collective-permute-start.3 = (bf16[32,256,128]{2,1,0:T(8,128)(2,1)}, bf16[32,256,128]{2,1,0:T(8,128)(2,1)S(1)}, u32[]{:S(2)}, u32[]{:S(2)}) collective-permute-start(bf16[32,256,128]{2,1,0:T(8,128)(2,1)} %collective-permute-done.2.refs_0_), channel_id=1, source_target_pairs={{0,4},{2,6},{4,8},{6,10},{8,12},{10,14},{12,0},{14,2},{1,5},{3,7},... | collective-permute-start | bytes 6291464 | tf_op jit(solution)/shard_map/ppermute | solution.py:135
  100.2 93.0 %collective-permute-start.10 = (bf16[32,256,128]{2,1,0:T(8,128)(2,1)}, bf16[32,256,128]{2,1,0:T(8,128)(2,1)}, u32[]{:S(2)}, u32[]{:S(2)}) collective-permute-start(bf16[32,256,128]{2,1,0:T(8,128)(2,1)} %collective-permute-done.2.refs_0_), channel_id=1, source_target_pairs={{0,2},{2,0},{4,6},{6,4},{8,10},{10,8},{12,14},{14,12},{1,3},{3,1},... | collective-permute-start | bytes 6291464 | tf_op jit(solution)/shard_map/ppermute | solution.py:140
  191.4 92.3 %collective-permute-start.12 = (bf16[32,256,128]{2,1,0:T(8,128)(2,1)S(1)}, bf16[32,256,128]{2,1,0:T(8,128)(2,1)S(1)}, u32[]{:S(2)}, u32[]{:S(2)}) collective-permute-start(bf16[32,256,128]{2,1,0:T(8,128)(2,1)S(1)} %collective-permute-done.3.refs_0_), channel_id=1, source_target_pairs={{0,4},{2,6},{4,8},{6,10},{8,12},{10,14},{12,0},{14,2},{1,5},{3,7},... | collective-permute-start | bytes 6291464 | tf_op jit(solution)/shard_map/ppermute | solution.py:135
  191.4 93.3 %collective-permute-start.6 = (bf16[32,256,128]{2,1,0:T(8,128)(2,1)S(1)}, bf16[32,256,128]{2,1,0:T(8,128)(2,1)}, u32[]{:S(2)}, u32[]{:S(2)}) collective-permute-start(bf16[32,256,128]{2,1,0:T(8,128)(2,1)S(1)} %collective-permute-done.3.refs_0_), channel_id=1, source_target_pairs={{0,2},{2,0},{4,6},{6,4},{8,10},{10,8},{12,14},{14,12},{1,3},{3,1},... | collective-permute-start | bytes 6291464 | tf_op jit(solution)/shard_map/ppermute | solution.py:140
  195.6 38.4 %copy-start.24 = (bf16[32,256,128]{2,1,0:T(8,128)(2,1)}, bf16[32,256,128]{2,1,0:T(8,128)(2,1)S(1)}, u32[]{:S(2)}) copy-start(bf16[32,256,128]{2,1,0:T(8,128)(2,1)S(1)} %collective-permute-done.5.refs_1_) | copy-start | bytes 6291460
  195.6 87.7 %collective-permute-start.13 = (bf16[32,256,128]{2,1,0:T(8,128)(2,1)S(1)}, bf16[32,256,128]{2,1,0:T(8,128)(2,1)}, u32[]{:S(2)}, u32[]{:S(2)}) collective-permute-start(bf16[32,256,128]{2,1,0:T(8,128)(2,1)S(1)} %collective-permute-done.5.refs_1_), channel_id=1, source_target_pairs={{0,4},{2,6},{4,8},{6,10},{8,12},{10,14},{12,0},{14,2},{1,5},{3,7},... | collective-permute-start | bytes 6291464 | tf_op jit(solution)/shard_map/ppermute | solution.py:135
  195.6 89.1 %collective-permute-start.7 = (bf16[32,256,128]{2,1,0:T(8,128)(2,1)S(1)}, bf16[32,256,128]{2,1,0:T(8,128)(2,1)}, u32[]{:S(2)}, u32[]{:S(2)}) collective-permute-start(bf16[32,256,128]{2,1,0:T(8,128)(2,1)S(1)} %collective-permute-done.5.refs_1_), channel_id=1, source_target_pairs={{0,2},{2,0},{4,6},{6,4},{8,10},{10,8},{12,14},{14,12},{1,3},{3,1},... | collective-permute-start | bytes 6291464 | tf_op jit(solution)/shard_map/ppermute | solution.py:140
  283.2 52.6 %collective-permute-start.15 = (bf16[32,256,128]{2,1,0:T(8,128)(2,1)}, bf16[32,256,128]{2,1,0:T(8,128)(2,1)}, u32[]{:S(2)}, u32[]{:S(2)}) collective-permute-start(bf16[32,256,128]{2,1,0:T(8,128)(2,1)} %collective-permute-done.13.refs_1_), channel_id=1, source_target_pairs={{0,2},{2,0},{4,6},{6,4},{8,10},{10,8},{12,14},{14,12},{1,3},{3,1},... | collective-permute-start | bytes 6291464 | tf_op jit(solution)/shard_map/ppermute | solution.py:140
  283.7 88.8 %collective-permute-start.14 = (bf16[32,256,128]{2,1,0:T(8,128)(2,1)S(1)}, bf16[32,256,128]{2,1,0:T(8,128)(2,1)}, u32[]{:S(2)}, u32[]{:S(2)}) collective-permute-start(bf16[32,256,128]{2,1,0:T(8,128)(2,1)S(1)} %collective-permute-done.12.refs_0_), channel_id=1, source_target_pairs={{0,2},{2,0},{4,6},{6,4},{8,10},{10,8},{12,14},{14,12},{1,3},{3,1},... | collective-permute-start | bytes 6291464 | tf_op jit(solution)/shard_map/ppermute | solution.py:140
  284.7 36.5 %copy-start.6 = (f32[128,64,128]{2,1,0:T(8,128)S(1)}, f32[128,64,128]{2,1,0:T(8,128)}, u32[]{:S(2)}) copy-start(f32[128,64,128]{2,1,0:T(8,128)} %shard_map.100) | copy-start | bytes 12582916
  321.2 10.5 %copy-start.21 = (bf16[32,64,128]{2,1,0:T(8,128)(2,1)S(1)}, bf16[32,64,128]{2,1,0:T(8,128)(2,1)}, u32[]{:S(2)}) copy-start(bf16[32,64,128]{2,1,0:T(8,128)(2,1)} %constant_dynamic-slice_fusion.11) | copy-start | bytes 1572868
  323.7 97.4 %collective-permute-start.9 = (bf16[128,64,128]{2,1,0:T(8,128)(2,1)}, bf16[128,64,128]{2,1,0:T(8,128)(2,1)}, u32[]{:S(2)}, u32[]{:S(2)}) collective-permute-start(bf16[128,64,128]{2,1,0:T(8,128)(2,1)} %select_convert_fusion.1), channel_id=1, source_target_pairs={{0,1},{1,0},{2,3},{3,2},{4,5},{5,4},{6,7},{7,6},{8,9},{9,8},{10,11... | collective-permute-start | bytes 6291464 | tf_op jit(solution)/shard_map/ppermute | solution.py:143
  334.6 39.3 %copy-start.9 = (bf16[64,64,128]{2,1,0:T(8,128)(2,1)S(1)}, bf16[64,64,128]{2,1,0:T(8,128)(2,1)}, u32[]{:S(2)}) copy-start(bf16[64,64,128]{2,1,0:T(8,128)(2,1)} %get-tuple-element.16) | copy-start | bytes 3145732
  334.6 89.6 %collective-permute-start.8 = (bf16[128,64,128]{2,1,0:T(8,128)(2,1)}, bf16[128,64,128]{2,1,0:T(8,128)(2,1)}, u32[]{:S(2)}, u32[]{:S(2)}) collective-permute-start(bf16[128,64,128]{2,1,0:T(8,128)(2,1)} %broadcast_select_fusion.1), channel_id=1, source_target_pairs={{0,1},{1,0},{2,3},{3,2},{4,5},{5,4},{6,7},{7,6},{8,9},{9,8},{10,11... | collective-permute-start | bytes 6291464 | tf_op jit(solution)/shard_map/ppermute | solution.py:143
  375.8 60.1 %collective-permute-start.16 = (bf16[128,64,128]{2,1,0:T(8,128)(2,1)}, bf16[128,64,128]{2,1,0:T(8,128)(2,1)}, u32[]{:S(2)}, u32[]{:S(2)}) collective-permute-start(bf16[128,64,128]{2,1,0:T(8,128)(2,1)} %broadcast_select_fusion), channel_id=1, source_target_pairs={{0,1},{1,0},{2,3},{3,2},{4,5},{5,4},{6,7},{7,6},{8,9},{9,8},{10,11... | collective-permute-start | bytes 6291464 | tf_op jit(solution)/shard_map/ppermute | solution.py:143
  379.8 36.5 %copy-start.5 = (f32[128,64,128]{2,1,0:T(8,128)S(1)}, f32[128,64,128]{2,1,0:T(8,128)}, u32[]{:S(2)}) copy-start(f32[128,64,128]{2,1,0:T(8,128)} %shard_map.102) | copy-start | bytes 12582916
  421.1 26.3 %collective-permute-start.17 = (bf16[128,64,128]{2,1,0:T(8,128)(2,1)}, bf16[128,64,128]{2,1,0:T(8,128)(2,1)}, u32[]{:S(2)}, u32[]{:S(2)}) collective-permute-start(bf16[128,64,128]{2,1,0:T(8,128)(2,1)} %select_convert_fusion), channel_id=1, source_target_pairs={{0,1},{1,0},{2,3},{3,2},{4,5},{5,4},{6,7},{7,6},{8,9},{9,8},{10,11... | collective-permute-start | bytes 6291464 | tf_op jit(solution)/shard_map/ppermute | solution.py:143
  439.6 7.8 %copy-start.4 = (bf16[128,64,128]{2,1,0:T(8,128)(2,1)}, bf16[128,64,128]{2,1,0:T(8,128)(2,1)S(1)}, u32[]{:S(2)}) copy-start(bf16[128,64,128]{2,1,0:T(8,128)(2,1)S(1)} %get-tuple-element.8) | copy-start | bytes 6291460
  439.6 7.8 %copy-start.7 = (f32[128,64,128]{2,1,0:T(8,128)S(1)}, f32[128,64,128]{2,1,0:T(8,128)}, u32[]{:S(2)}) copy-start(f32[128,64,128]{2,1,0:T(8,128)} %shard_map.103) | copy-start | bytes 12582916
  454.3 9.2 %copy-start.30 = (bf16[128,128]{1,0:T(8,128)(2,1)S(1)}, bf16[128,128]{1,0:T(8,128)(2,1)}, u32[]{:S(2)}) copy-start(bf16[128,128]{1,0:T(8,128)(2,1)} %param.19) | copy-start | bytes 98308
  (17 other events, 72.3 us)

commit v4 on v3

--- a/solution.py
+++ b/solution.py
@@ -170,6 +170,22 @@
     def source_pair(d):
         return lax.rem(pair_at - d + n_pairs, n_pairs)
 
+    def halves(d):
+        mine_at = source_pair(d) * width + side_at * rows_tile
+        other_at = source_pair(d) * width + (1 - side_at) * rows_tile
+        return (mine, mine_at), (other, other_at)
+
+    def product_of(d, held, first_row, spot):
+        rows_mask = lax.dynamic_slice_in_dim(mask_values, first_row, rows_tile)
+        return left_product(
+            [held[d, n] for n in range(CHUNKS)],
+            spot,
+            rows_mask[:, None] * mask_cols[None, :],
+            in_gain[None],
+            left_weight,
+            right_side,
+        )
+
     def product(d):
         rows_mask = lax.dynamic_slice_in_dim(mask_values, source_pair(d) * width, width)
         blocks = [mine[d, n] for n in range(CHUNKS)] + [other[d, n] for n in range(CHUNKS)]
@@ -182,6 +198,16 @@
             right_side,
         )
 
+    def last_product(d, earlier):
+        start = jnp.zeros((1,), jnp.int32)
+        later = lax.optimization_barrier((start, earlier))[0]
+        (held, held_at), (swapped, swapped_at) = halves(d)
+        held_sum = product_of(d, held, held_at, start)
+        swapped_sum = product_of(d, swapped, swapped_at, later)
+        first = jnp.where(side_at == 0, held_sum, swapped_sum)
+        second = jnp.where(side_at == 0, swapped_sum, held_sum)
+        return jnp.concatenate([first, second], axis=2)
+
     column_at = lax.rem(row_at * rows_tile, cols_tile)
     column_core = (row_at * rows_tile) // cols_tile
 
@@ -197,7 +223,7 @@
         second = jnp.where(side_at == 0, swapped, held)
         return jnp.concatenate([first, second], axis=0)
 
-    products = [product(d) for d in range(n_pairs)]
+    products = [product(d) for d in range(n_pairs - 1)]
     out = jnp.zeros((rows_tile, cols_tile, channels), jnp.bfloat16)
     for d in range(half_pairs):
         keep_near = source_pair(d) // half_pairs == col_at
@@ -210,6 +236,8 @@
                 "ijd,dc->jic", normalise(turned), out_gate, preferred_element_type=jnp.float32
             )
         )
+        if d == half_pairs - 1:
+            products.append(last_product(n_pairs - 1, out))
         near_sum, far_sum = products[d], products[d + half_pairs]
         got_sum = sibling(jnp.where(keep_near, far_sum, near_sum).astype(jnp.bfloat16))
         combined = jnp.where(keep_near, near_sum, far_sum) + got_sum.astype(jnp.float32)

time: 479 us -> 492 us (1.027); the launches traced: 477 us -> 484 us
  Pallas kernels: 146 us -> 155 us
  matrix products: 32.5 us -> 23.9 us
  other arithmetic: 54.1 us -> 59.4 us
  waiting for transfers between devices: 169 us -> 174 us
    ppermute x8, waiting for transfers between devices: 35.6 us -> 93.9 us  [across(): return lax.ppermute(block, 'rows', [(r, r ^ 1) for r in range(n_rows)])]
    ppermute x6, waiting for transfers between devices: 134 us -> 79.8 us  [along(): lax.ppermute(block, 'rows', [(r, (r + 2 * step) % n_rows) for r in range(...]
    pallas_call x4 -> x5, Pallas kernels: 146 us -> 155 us  [left_product(): pl.pallas_call(functools.partial(left_kernel, parts, steps), grid_spec=pl...]
    dot_general x2, matrix products: 9.82 us -> 4.74 us  [body(): jnp.einsum('ijd,dc->jic', normalise(turned), out_gate, preferred_element_...]
  transfers between devices with their start and end apart: 18 -> 18, of which waited for: 4 -> 6; matrix products, arithmetic and copies ran while one was open for 22% -> 23% of each run, Pallas kernels for 31% -> 27%
where the time goes in v4:
time: 492 us; the launch traced here: 484 us
  waiting for transfers between devices  174 us (35%)
  Pallas kernels  155 us (32%)
  other arithmetic  59.4 us (12%)
  local copies, waits for them, and re-layouts  53.1 us (11%)
  matrix products  23.9 us (5%)
  starting transfers between devices  17.5 us (4%)
    pallas_call x5, Pallas kernels, left_product(): pl.pallas_call(functools.partial(left_kernel, parts, steps), grid_spec=pl...  155 us
    ppermute x8, waiting for transfers between devices, across(): return lax.ppermute(block, 'rows', [(r, r ^ 1) for r in range(n_rows)])  93.9 us
    ppermute x6, waiting for transfers between devices, along(): lax.ppermute(block, 'rows', [(r, (r + 2 * step) % n_rows) for r in range(...  79.8 us
    dynamic_slice x15, local copies, waits for them, and re-layouts, cut(): lax.dynamic_slice_in_dim(c, column_at, rows_tile, 1)  15.8 us
    reduce_sum x3, other arithmetic, norm_last(): spread = jnp.mean(centred * centred, axis=-1, keepdims=True)  12.1 us
    reduce_sum x3, other arithmetic, norm_last(): average = jnp.mean(values, axis=-1, keepdims=True)  10.8 us
    reduce_sum x2, other arithmetic, norm_first(): average = jnp.mean(values, axis=0, keepdims=True)  9.95 us
  transfers between devices with their start and end apart: 18, of which 6 were waited for; matrix products, arithmetic and copies ran while one was open for 23% of the time, Pallas kernels for 27%

profile of v4, /device:TPU:1, one launch (start us, length us, event | category | flops | bytes accessed | tf_op | source)
XLA Modules:
  0.0 483.8 jit_solution(15325777653604525360)
XLA Ops:
  0.0 4.0 fusion.42
  8.9 3.4 convert_reduce_fusion
  12.4 6.1 %fusion.2 = f32[64,256]{1,0:T(8,128)S(1)} fusion(bf16[64,256,128]{2,1,0:T(8,128)(2,1)} %param.10, f32[64,256]{1,0:T(8,128)S(1)} %broadcast_multiply_fusion.6), kind=kLoop, calls=%fused_computation.4 | loop fusion | flops 8372224 | bytes 4325376 | tf_op jit(solution)/shard_map/reduce_sum | solution.py:98
  18.6 7.8 %fusion.22 = f32[64,256,128]{2,1,0:T(8,128)} fusion(bf16[64,256,128]{2,1,0:T(8,128)(2,1)S(1)} %copy-done.3, f32[128]{0:T(128)S(1)} %copy-done.2, f32[64,256]{1,0:T(8,128)S(1)} %add_rsqrt_fusion.1, f32[64,256]{1,0:T(8,128)S(1)} %broadcast_multiply_fusion.6, bf16[128,128]{1,0:T(8,128)(2,1)S(1)} %copy-done), kind=kOutput, calls=%fused_computation.41 | convolution fusion | flops 547356672 | bytes 12747264 | tf_op jit(solution)/shard_map/xkd,dh->hxk/dot_general | solution.py:155
  26.5 9.3 %copy.15 = f32[64,256,128]{1,0,2:T(8,128)} copy(f32[64,256,128]{2,1,0:T(8,128)} %fusion.22) | data formatting | bytes 16777216 | tf_op jit(solution)/shard_map/xkd,dh->hxk/dot_general | solution.py:155
  35.8 8.6 %fusion.20 = f32[64,256,128]{2,1,0:T(8,128)} fusion(bf16[64,256,128]{2,1,0:T(8,128)(2,1)} %param.10, f32[128]{0:T(128)S(1)} %copy-done.2, f32[64,256]{1,0:T(8,128)S(1)} %add_rsqrt_fusion.1, f32[64,256]{1,0:T(8,128)S(1)} %broadcast_multiply_fusion.6, bf16[128,128]{1,0:T(8,128)(2,1)S(1)} %copy-done.23), kind=kOutput, calls=%fused_computation.40 | convolution fusion | flops 547356672 | bytes 12747264 | tf_op jit(solution)/shard_map/xkd,dh->hxk/dot_general | solution.py:154
  44.4 9.3 %copy.16 = f32[64,256,128]{1,0,2:T(8,128)} copy(f32[64,256,128]{2,1,0:T(8,128)} %fusion.20) | data formatting | bytes 16777216 | tf_op jit(solution)/shard_map/xkd,dh->hxk/dot_general | solution.py:154
  56.6 8.7 %fusion.19.refs_7_.refs_5_ = bf16[128,64,256]{2,1,0:T(8,128)(2,1)} fusion(f32[64,256]{1,0:T(8,128)S(1)} %get-tuple-element.35, f32[64,256,128]{1,0,2:T(8,128)} %copy.16, f32[64,256,128]{1,0,2:T(8,128)} %copy.15), kind=kLoop, calls=%fused_computation.39 | loop fusion | flops 12582912 | bytes 21037056 | tf_op jit(solution)/shard_map/convert_element_type | solution.py:156
  67.9 30.7 %collective-permute-done.4.refs_1_ = bf16[32,256,128]{2,1,0:T(8,128)(2,1)} collective-permute-done((bf16[32,256,128]{2,1,0:T(8,128)(2,1)}, bf16[32,256,128]{2,1,0:T(8,128)(2,1)}, u32[]{:S(2)}, u32[]{:S(2)}) %collective-permute-start.4) | collective-permute-done | bytes 2097184 | tf_op jit(solution)/shard_map/ppermute | solution.py:135
  99.6 36.4 %shard_map.100 = f32[128,64,128]{2,1,0:T(8,128)} custom-call(s32[1]{0:T(128)} %bitcast.3.place_ref, bf16[32,256,128]{2,1,0:T(8,128)(2,1)S(1)} %get-tuple-element.17.refs_0_, bf16[32,256,128]{2,1,0:T(8,128)(2,1)} %get-tuple-element.18.refs_1_, bf16[32,256,128]{2,1,0:T(8,128)(2,1)} %collective-permute-done.refs_2_, ...), custom_call_target="tpu_custom_call" | custom-call | flops 42949672960 | bytes 20971520 | tf_op jit(solution)/shard_map/pallas_call | solution.py:69
  138.4 5.0 %collective-permute-done.3.refs_0_ = bf16[32,256,128]{2,1,0:T(8,128)(2,1)S(1)} collective-permute-done((bf16[32,256,128]{2,1,0:T(8,128)(2,1)}, bf16[32,256,128]{2,1,0:T(8,128)(2,1)S(1)}, u32[]{:S(2)}, u32[]{:S(2)}) %collective-permute-start.3) | collective-permute-done | bytes 2097184 | tf_op jit(solution)/shard_map/ppermute | solution.py:135
  144.4 44.0 %collective-permute-done.5.refs_1_ = bf16[32,256,128]{2,1,0:T(8,128)(2,1)} collective-permute-done((bf16[32,256,128]{2,1,0:T(8,128)(2,1)}, bf16[32,256,128]{2,1,0:T(8,128)(2,1)}, u32[]{:S(2)}, u32[]{:S(2)}) %collective-permute-start.5) | collective-permute-done | bytes 2097184 | tf_op jit(solution)/shard_map/ppermute | solution.py:135
  190.9 36.7 %shard_map.102 = f32[128,64,128]{2,1,0:T(8,128)} custom-call(s32[1]{0:T(128)} %bitcast.3.place_ref, bf16[32,256,128]{2,1,0:T(8,128)(2,1)} %collective-permute-done.2.refs_0_, bf16[32,256,128]{2,1,0:T(8,128)(2,1)} %collective-permute-done.4.refs_1_, bf16[32,256,128]{2,1,0:T(8,128)(2,1)} %collective-permute-done.10.refs_2_, ...), custom_call_target="tpu_custom_call" | custom-call | flops 42949672960 | bytes 20971520 | tf_op jit(solution)/shard_map/pallas_call | solution.py:69
  227.6 4.5 collective-permute-done.6.refs_2_
  232.1 45.0 %collective-permute-done.7.refs_3_ = bf16[32,256,128]{2,1,0:T(8,128)(2,1)} collective-permute-done((bf16[32,256,128]{2,1,0:T(8,128)(2,1)}, bf16[32,256,128]{2,1,0:T(8,128)(2,1)}, u32[]{:S(2)}, u32[]{:S(2)}) %collective-permute-start.7) | collective-permute-done | bytes 2097184 | tf_op jit(solution)/shard_map/ppermute | solution.py:140
  277.2 36.5 %shard_map.101 = f32[128,64,128]{2,1,0:T(8,128)} custom-call(s32[1]{0:T(128)} %bitcast.3.place_ref, bf16[32,256,128]{2,1,0:T(8,128)(2,1)S(1)} %collective-permute-done.3.refs_0_, bf16[32,256,128]{2,1,0:T(8,128)(2,1)} %collective-permute-done.5.refs_1_, bf16[32,256,128]{2,1,0:T(8,128)(2,1)} %copy-done.22, ...), custom_call_target="tpu_custom_call" | custom-call | flops 42949672960 | bytes 20971520 | tf_op jit(solution)/shard_map/pallas_call | solution.py:69
  313.6 2.4 select_convert_fusion.1
  316.1 4.0 collective-permute-start.9
  325.9 22.4 %shard_map.103 = f32[128,64,64]{2,1,0:T(8,128)} custom-call(s32[1]{0:T(128)} %constant.114.clone.1.place_ref, bf16[32,256,128]{2,1,0:T(8,128)(2,1)S(1)} %collective-permute-done.12.refs_0_, bf16[32,256,128]{2,1,0:T(8,128)(2,1)} %collective-permute-done.13.refs_1_, f32[64,256]{1,0:T(8,128)S(1)} %get-tuple-element.33.refs_2_, f32[1,128]{1,0:T(1,128)S(1)} %bitcast.47, ...), custom_call_target="tpu_custom_call" | custom-call | flops 21474836480 | bytes 20971520 | tf_op jit(solution)/shard_map/pallas_call | solution.py:69
  348.3 3.3 fusion.41
  354.2 4.6 copy.27
  358.8 3.7 convert_reduce_fusion.2
  362.6 2.9 fusion.12
  371.8 44.4 %collective-permute-done.15.refs_1_ = bf16[32,256,128]{2,1,0:T(8,128)(2,1)} collective-permute-done((bf16[32,256,128]{2,1,0:T(8,128)(2,1)}, bf16[32,256,128]{2,1,0:T(8,128)(2,1)}, u32[]{:S(2)}, u32[]{:S(2)}) %collective-permute-start.15) | collective-permute-done | bytes 2097184 | tf_op jit(solution)/shard_map/ppermute | solution.py:140
  416.2 23.0 %shard_map.104 = f32[128,64,64]{2,1,0:T(8,128)} custom-call(s32[1]{0:T(128)} %constant.114.clone.1.place_ref, bf16[32,256,128]{2,1,0:T(8,128)(2,1)} %collective-permute-done.14.refs_0_, bf16[32,256,128]{2,1,0:T(8,128)(2,1)} %collective-permute-done.15.refs_1_, f32[64,256]{1,0:T(8,128)S(1)} %get-tuple-element.34.refs_2_, f32[1,128]{1,0:T(1,128)S(1)} %bitcast.48, ...), custom_call_target="tpu_custom_call" | custom-call | flops 21474836480 | bytes 20971520 | tf_op jit(solution)/shard_map/pallas_call | solution.py:69
  439.2 3.9 broadcast_select_fusion.1
  443.1 3.0 select_convert_fusion
  458.8 6.7 %fusion.40 = (f32[64,128]{1,0:T(8,128)S(1)}, f32[128,64,128]{2,1,0:T(8,128)S(1)}) fusion(bf16[128,64,128]{2,1,0:T(8,128)(2,1)} %collective-permute-done.17, f32[128,64,128]{2,1,0:T(8,128)} %shard_map.102, f32[128,64,64]{2,1,0:T(8,128)} %copy-done.5, f32[128,64,64]{2,1,0:T(8,128)} %copy-done.4, pred[]{:T(512)S(6)} %eq.13), kind=kLoop, calls=%fused_computation.117 | loop fusion | flops 5234688 | bytes 14712833 | tf_op jit(solution)/shard_map/reduce_sum | solution.py:103
  466.7 3.4 copy.31
  470.1 3.7 convert_reduce_fusion.1
  473.9 3.0 fusion.9
  480.7 2.7 copy_dynamic-update-slice_fusion
  (137 shorter events, 49.4 us)
Async XLA Ops:
  0.0 18.6 %copy-start = (bf16[128,128]{1,0:T(8,128)(2,1)S(1)}, bf16[128,128]{1,0:T(8,128)(2,1)}, u32[]{:S(2)}) copy-start(bf16[128,128]{1,0:T(8,128)(2,1)} %param.16) | copy-start | bytes 98308
  4.0 61.3 %collective-permute-start.2 = (bf16[32,256,128]{2,1,0:T(8,128)(2,1)S(1)}, bf16[32,256,128]{2,1,0:T(8,128)(2,1)}, u32[]{:S(2)}, u32[]{:S(2)}) collective-permute-start(bf16[32,256,128]{2,1,0:T(8,128)(2,1)S(1)} %get-tuple-element.17.refs_0_), channel_id=1, source_target_pairs={{0,4},{2,6},{4,8},{6,10},{8,12},{10,14},{12,0},{14,2},{1,5},{3,7},... | collective-permute-start | bytes 6291464 | tf_op jit(solution)/shard_map/ppermute | solution.py:135
  6.2 92.4 %collective-permute-start = (bf16[32,256,128]{2,1,0:T(8,128)(2,1)S(1)}, bf16[32,256,128]{2,1,0:T(8,128)(2,1)}, u32[]{:S(2)}, u32[]{:S(2)}) collective-permute-start(bf16[32,256,128]{2,1,0:T(8,128)(2,1)S(1)} %get-tuple-element.17.refs_0_), channel_id=1, source_target_pairs={{0,2},{2,0},{4,6},{6,4},{8,10},{10,8},{12,14},{14,12},{1,3},{3,1},... | collective-permute-start | bytes 6291464 | tf_op jit(solution)/shard_map/ppermute | solution.py:140
  7.4 91.2 %collective-permute-start.4 = (bf16[32,256,128]{2,1,0:T(8,128)(2,1)}, bf16[32,256,128]{2,1,0:T(8,128)(2,1)}, u32[]{:S(2)}, u32[]{:S(2)}) collective-permute-start(bf16[32,256,128]{2,1,0:T(8,128)(2,1)} %get-tuple-element.18.refs_1_), channel_id=1, source_target_pairs={{0,4},{2,6},{4,8},{6,10},{8,12},{10,14},{12,0},{14,2},{1,5},{3,7},... | collective-permute-start | bytes 6291464 | tf_op jit(solution)/shard_map/ppermute | solution.py:135
  8.7 90.9 %collective-permute-start.1 = (bf16[32,256,128]{2,1,0:T(8,128)(2,1)}, bf16[32,256,128]{2,1,0:T(8,128)(2,1)}, u32[]{:S(2)}, u32[]{:S(2)}) collective-permute-start(bf16[32,256,128]{2,1,0:T(8,128)(2,1)} %get-tuple-element.18.refs_1_), channel_id=1, source_target_pairs={{0,2},{2,0},{4,6},{6,4},{8,10},{10,8},{12,14},{14,12},{1,3},{3,1},... | collective-permute-start | bytes 6291464 | tf_op jit(solution)/shard_map/ppermute | solution.py:140
  8.9 9.7 %copy-start.2 = (f32[128]{0:T(128)S(1)}, f32[128]{0:T(128)}, u32[]{:S(2)}) copy-start(f32[128]{0:T(128)} %param.12) | copy-start | bytes 1540
  26.5 9.3 %copy-start.23 = (bf16[128,128]{1,0:T(8,128)(2,1)S(1)}, bf16[128,128]{1,0:T(8,128)(2,1)}, u32[]{:S(2)}) copy-start(bf16[128,128]{1,0:T(8,128)(2,1)} %param.15) | copy-start | bytes 98308
  44.3 9.3 %copy-start.24 = (bf16[128,128]{1,0:T(8,128)(2,1)S(1)}, bf16[128,128]{1,0:T(8,128)(2,1)}, u32[]{:S(2)}) copy-start(bf16[128,128]{1,0:T(8,128)(2,1)} %param.13) | copy-start | bytes 98308
  44.3 9.4 %copy-start.25 = (bf16[128,128]{1,0:T(8,128)(2,1)S(1)}, bf16[128,128]{1,0:T(8,128)(2,1)}, u32[]{:S(2)}) copy-start(bf16[128,128]{1,0:T(8,128)(2,1)} %param.14) | copy-start | bytes 98308
  65.4 78.1 %collective-permute-start.3 = (bf16[32,256,128]{2,1,0:T(8,128)(2,1)}, bf16[32,256,128]{2,1,0:T(8,128)(2,1)S(1)}, u32[]{:S(2)}, u32[]{:S(2)}) collective-permute-start(bf16[32,256,128]{2,1,0:T(8,128)(2,1)} %collective-permute-done.2.refs_0_), channel_id=1, source_target_pairs={{0,4},{2,6},{4,8},{6,10},{8,12},{10,14},{12,0},{14,2},{1,5},{3,7},... | collective-permute-start | bytes 6291464 | tf_op jit(solution)/shard_map/ppermute | solution.py:135
  66.7 124.0 %collective-permute-start.10 = (bf16[32,256,128]{2,1,0:T(8,128)(2,1)}, bf16[32,256,128]{2,1,0:T(8,128)(2,1)}, u32[]{:S(2)}, u32[]{:S(2)}) collective-permute-start(bf16[32,256,128]{2,1,0:T(8,128)(2,1)} %collective-permute-done.2.refs_0_), channel_id=1, source_target_pairs={{0,2},{2,0},{4,6},{6,4},{8,10},{10,8},{12,14},{14,12},{1,3},{3,1},... | collective-permute-start | bytes 6291464 | tf_op jit(solution)/shard_map/ppermute | solution.py:140
  98.6 89.9 %collective-permute-start.5 = (bf16[32,256,128]{2,1,0:T(8,128)(2,1)}, bf16[32,256,128]{2,1,0:T(8,128)(2,1)}, u32[]{:S(2)}, u32[]{:S(2)}) collective-permute-start(bf16[32,256,128]{2,1,0:T(8,128)(2,1)} %collective-permute-done.4.refs_1_), channel_id=1, source_target_pairs={{0,4},{2,6},{4,8},{6,10},{8,12},{10,14},{12,0},{14,2},{1,5},{3,7},... | collective-permute-start | bytes 6291464 | tf_op jit(solution)/shard_map/ppermute | solution.py:135
  98.6 92.3 %collective-permute-start.11 = (bf16[32,256,128]{2,1,0:T(8,128)(2,1)}, bf16[32,256,128]{2,1,0:T(8,128)(2,1)}, u32[]{:S(2)}, u32[]{:S(2)}) collective-permute-start(bf16[32,256,128]{2,1,0:T(8,128)(2,1)} %collective-permute-done.4.refs_1_), channel_id=1, source_target_pairs={{0,2},{2,0},{4,6},{6,4},{8,10},{10,8},{12,14},{14,12},{1,3},{3,1},... | collective-permute-start | bytes 6291464 | tf_op jit(solution)/shard_map/ppermute | solution.py:140
  99.6 38.6 %copy-start.17 = (bf16[32,64,128]{2,1,0:T(8,128)(2,1)S(1)}, bf16[32,64,128]{2,1,0:T(8,128)(2,1)}, u32[]{:S(2)}) copy-start(bf16[32,64,128]{2,1,0:T(8,128)(2,1)} %get-tuple-element.39) | copy-start | bytes 1572868
  99.6 38.6 %copy-start.18 = (bf16[32,64,128]{2,1,0:T(8,128)(2,1)S(1)}, bf16[32,64,128]{2,1,0:T(8,128)(2,1)}, u32[]{:S(2)}) copy-start(bf16[32,64,128]{2,1,0:T(8,128)(2,1)} %get-tuple-element.40) | copy-start | bytes 1572868
  138.4 184.1 %copy-start.9 = (bf16[64,64,128]{2,1,0:T(8,128)(2,1)}, bf16[64,64,128]{2,1,0:T(8,128)(2,1)S(1)}, u32[]{:S(2)}) copy-start(bf16[64,64,128]{2,1,0:T(8,128)(2,1)S(1)} %get-tuple-element.24) | copy-start | bytes 3145732
  143.4 88.7 %collective-permute-start.6 = (bf16[32,256,128]{2,1,0:T(8,128)(2,1)S(1)}, bf16[32,256,128]{2,1,0:T(8,128)(2,1)S(1)}, u32[]{:S(2)}, u32[]{:S(2)}) collective-permute-start(bf16[32,256,128]{2,1,0:T(8,128)(2,1)S(1)} %collective-permute-done.3.refs_0_), channel_id=1, source_target_pairs={{0,2},{2,0},{4,6},{6,4},{8,10},{10,8},{12,14},{14,12},{1,3},{3,1},... | collective-permute-start | bytes 6291464 | tf_op jit(solution)/shard_map/ppermute | solution.py:140
  144.4 180.0 %collective-permute-start.12 = (bf16[32,256,128]{2,1,0:T(8,128)(2,1)S(1)}, bf16[32,256,128]{2,1,0:T(8,128)(2,1)S(1)}, u32[]{:S(2)}, u32[]{:S(2)}) collective-permute-start(bf16[32,256,128]{2,1,0:T(8,128)(2,1)S(1)} %collective-permute-done.3.refs_0_), channel_id=1, source_target_pairs={{0,4},{2,6},{4,8},{6,10},{8,12},{10,14},{12,0},{14,2},{1,5},{3,7},... | collective-permute-start | bytes 6291464 | tf_op jit(solution)/shard_map/ppermute | solution.py:135
  188.5 88.7 %collective-permute-start.7 = (bf16[32,256,128]{2,1,0:T(8,128)(2,1)}, bf16[32,256,128]{2,1,0:T(8,128)(2,1)}, u32[]{:S(2)}, u32[]{:S(2)}) collective-permute-start(bf16[32,256,128]{2,1,0:T(8,128)(2,1)} %collective-permute-done.5.refs_1_), channel_id=1, source_target_pairs={{0,2},{2,0},{4,6},{6,4},{8,10},{10,8},{12,14},{14,12},{1,3},{3,1},... | collective-permute-start | bytes 6291464 | tf_op jit(solution)/shard_map/ppermute | solution.py:140
  190.7 135.0 %collective-permute-start.13 = (bf16[32,256,128]{2,1,0:T(8,128)(2,1)}, bf16[32,256,128]{2,1,0:T(8,128)(2,1)}, u32[]{:S(2)}, u32[]{:S(2)}) collective-permute-start(bf16[32,256,128]{2,1,0:T(8,128)(2,1)} %collective-permute-done.5.refs_1_), channel_id=1, source_target_pairs={{0,4},{2,6},{4,8},{6,10},{8,12},{10,14},{12,0},{14,2},{1,5},{3,7},... | collective-permute-start | bytes 6291464 | tf_op jit(solution)/shard_map/ppermute | solution.py:135
  232.1 45.0 %copy-start.22 = (bf16[32,256,128]{2,1,0:T(8,128)(2,1)}, bf16[32,256,128]{2,1,0:T(8,128)(2,1)S(1)}, u32[]{:S(2)}) copy-start(bf16[32,256,128]{2,1,0:T(8,128)(2,1)S(1)} %collective-permute-done.6.refs_2_) | copy-start | bytes 6291460
  277.2 36.5 %copy-start.6 = (f32[128,64,128]{2,1,0:T(8,128)S(1)}, f32[128,64,128]{2,1,0:T(8,128)}, u32[]{:S(2)}) copy-start(f32[128,64,128]{2,1,0:T(8,128)} %shard_map.100) | copy-start | bytes 12582916
  316.1 32.3 %collective-permute-start.9 = (bf16[128,64,128]{2,1,0:T(8,128)(2,1)}, bf16[128,64,128]{2,1,0:T(8,128)(2,1)}, u32[]{:S(2)}, u32[]{:S(2)}) collective-permute-start(bf16[128,64,128]{2,1,0:T(8,128)(2,1)} %select_convert_fusion.1), channel_id=1, source_target_pairs={{0,1},{1,0},{2,3},{3,2},{4,5},{5,4},{6,7},{7,6},{8,9},{9,8},{10,11... | collective-permute-start | bytes 6291464 | tf_op jit(solution)/shard_map/ppermute | solution.py:143
  324.5 34.3 %collective-permute-start.8 = (bf16[128,64,128]{2,1,0:T(8,128)(2,1)}, bf16[128,64,128]{2,1,0:T(8,128)(2,1)}, u32[]{:S(2)}, u32[]{:S(2)}) collective-permute-start(bf16[128,64,128]{2,1,0:T(8,128)(2,1)} %broadcast_select_fusion.3), channel_id=1, source_target_pairs={{0,1},{1,0},{2,3},{3,2},{4,5},{5,4},{6,7},{7,6},{8,9},{9,8},{10,11... | collective-permute-start | bytes 6291464 | tf_op jit(solution)/shard_map/ppermute | solution.py:143
  324.5 47.4 %collective-permute-start.14 = (bf16[32,256,128]{2,1,0:T(8,128)(2,1)S(1)}, bf16[32,256,128]{2,1,0:T(8,128)(2,1)}, u32[]{:S(2)}, u32[]{:S(2)}) collective-permute-start(bf16[32,256,128]{2,1,0:T(8,128)(2,1)S(1)} %collective-permute-done.12.refs_0_), channel_id=1, source_target_pairs={{0,2},{2,0},{4,6},{6,4},{8,10},{10,8},{12,14},{14,12},{1,3},{3,1},... | collective-permute-start | bytes 6291464 | tf_op jit(solution)/shard_map/ppermute | solution.py:140
  325.7 90.5 %collective-permute-start.15 = (bf16[32,256,128]{2,1,0:T(8,128)(2,1)}, bf16[32,256,128]{2,1,0:T(8,128)(2,1)}, u32[]{:S(2)}, u32[]{:S(2)}) collective-permute-start(bf16[32,256,128]{2,1,0:T(8,128)(2,1)} %collective-permute-done.13.refs_1_), channel_id=1, source_target_pairs={{0,2},{2,0},{4,6},{6,4},{8,10},{10,8},{12,14},{14,12},{1,3},{3,1},... | collective-permute-start | bytes 6291464 | tf_op jit(solution)/shard_map/ppermute | solution.py:140
  325.9 22.4 %copy-start.7 = (f32[128,64,128]{2,1,0:T(8,128)S(1)}, f32[128,64,128]{2,1,0:T(8,128)}, u32[]{:S(2)}) copy-start(f32[128,64,128]{2,1,0:T(8,128)} %shard_map.101) | copy-start | bytes 12582916
  371.8 44.4 %copy-start.16 = (bf16[64,256,128]{2,1,0:T(8,128)(2,1)}, bf16[64,256,128]{2,1,0:T(8,128)(2,1)S(1)}, u32[]{:S(2)}) copy-start(bf16[64,256,128]{2,1,0:T(8,128)(2,1)S(1)} %copy_dynamic-update-slice_fusion.1) | copy-start | bytes 12582916
  416.2 23.0 %copy-start.15 = (f32[128,64,64]{2,1,0:T(8,128)S(1)}, f32[128,64,64]{2,1,0:T(8,128)}, u32[]{:S(2)}) copy-start(f32[128,64,64]{2,1,0:T(8,128)} %shard_map.103) | copy-start | bytes 6291460
  447.0 11.8 %collective-permute-start.17 = (bf16[128,64,128]{2,1,0:T(8,128)(2,1)}, bf16[128,64,128]{2,1,0:T(8,128)(2,1)}, u32[]{:S(2)}, u32[]{:S(2)}) collective-permute-start(bf16[128,64,128]{2,1,0:T(8,128)(2,1)} %select_convert_fusion), channel_id=1, source_target_pairs={{0,1},{1,0},{2,3},{3,2},{4,5},{5,4},{6,7},{7,6},{8,9},{9,8},{10,11... | collective-permute-start | bytes 6291464 | tf_op jit(solution)/shard_map/ppermute | solution.py:143
  456.8 8.7 %copy-start.11 = (bf16[64,64,128]{2,1,0:T(8,128)(2,1)}, bf16[64,64,128]{2,1,0:T(8,128)(2,1)S(1)}, u32[]{:S(2)}) copy-start(bf16[64,64,128]{2,1,0:T(8,128)(2,1)S(1)} %get-tuple-element.21) | copy-start | bytes 3145732
  458.8 11.3 %collective-permute-start.16 = (bf16[128,64,128]{2,1,0:T(8,128)(2,1)}, bf16[128,64,128]{2,1,0:T(8,128)(2,1)}, u32[]{:S(2)}, u32[]{:S(2)}) collective-permute-start(bf16[128,64,128]{2,1,0:T(8,128)(2,1)} %broadcast_select_fusion.2), channel_id=1, source_target_pairs={{0,1},{1,0},{2,3},{3,2},{4,5},{5,4},{6,7},{7,6},{8,9},{9,8},{10,11... | collective-permute-start | bytes 6291464 | tf_op jit(solution)/shard_map/ppermute | solution.py:143
  (15 other events, 72.6 us)

commit v5 on v4

--- a/solution.py
+++ b/solution.py
@@ -189,9 +189,13 @@
     def product(d):
         rows_mask = lax.dynamic_slice_in_dim(mask_values, source_pair(d) * width, width)
         blocks = [mine[d, n] for n in range(CHUNKS)] + [other[d, n] for n in range(CHUNKS)]
+        spot = place
+        if d == n_pairs - 2:
+            arrived = [mine[d + 1, n] for n in range(CHUNKS)]
+            spot = lax.optimization_barrier((place, *arrived))[0]
         return left_product(
             blocks,
-            place,
+            spot,
             rows_mask[:, None] * mask_cols[None, :],
             in_gain[None],
             left_weight,

time: 492 us -> 493 us (level)
    ppermute x6, waiting for transfers between devices: 79.8 us -> 130 us  [along(): lax.ppermute(block, 'rows', [(r, (r + 2 * step) % n_rows) for r in range(...]
    ppermute x8, waiting for transfers between devices: 93.9 us -> 44.4 us  [across(): return lax.ppermute(block, 'rows', [(r, r ^ 1) for r in range(n_rows)])]
  transfers between devices with their start and end apart: 18 -> 18, of which waited for: 6 -> 5; matrix products, arithmetic and copies ran while one was open for 23% -> 22% of each run, Pallas kernels for 27% -> 20%
where the time goes in v5:
time: 493 us; the launch traced here: 484 us
  waiting for transfers between devices  175 us (35%)
  Pallas kernels  155 us (31%)
  other arithmetic  59.3 us (12%)
  local copies, waits for them, and re-layouts  53.4 us (11%)
  matrix products  23.9 us (5%)
  starting transfers between devices  16.9 us (3%)
    pallas_call x5, Pallas kernels, left_product(): pl.pallas_call(functools.partial(left_kernel, parts, steps), grid_spec=pl...  155 us
    ppermute x6, waiting for transfers between devices, along(): lax.ppermute(block, 'rows', [(r, (r + 2 * step) % n_rows) for r in range(...  130 us
    ppermute x8, waiting for transfers between devices, across(): return lax.ppermute(block, 'rows', [(r, r ^ 1) for r in range(n_rows)])  44.4 us
    dynamic_slice x15, local copies, waits for them, and re-layouts, cut(): lax.dynamic_slice_in_dim(c, column_at, rows_tile, 1)  15.8 us
    reduce_sum x3, other arithmetic, norm_last(): spread = jnp.mean(centred * centred, axis=-1, keepdims=True)  12.1 us
    reduce_sum x3, other arithmetic, norm_last(): average = jnp.mean(values, axis=-1, keepdims=True)  10.8 us
    reduce_sum x2, other arithmetic, norm_first(): average = jnp.mean(values, axis=0, keepdims=True)  9.95 us
  transfers between devices with their start and end apart: 18, of which 5 were waited for; matrix products, arithmetic and copies ran while one was open for 22% of the time, Pallas kernels for 20%

profile of v5, /device:TPU:1, one launch (start us, length us, event | category | flops | bytes accessed | tf_op | source)
XLA Modules:
  0.0 484.3 jit_solution(3380208713934749500)
XLA Ops:
  0.0 4.0 fusion.42
  8.9 3.4 convert_reduce_fusion
  12.4 6.1 %fusion.2 = f32[64,256]{1,0:T(8,128)S(1)} fusion(bf16[64,256,128]{2,1,0:T(8,128)(2,1)} %param.10, f32[64,256]{1,0:T(8,128)S(1)} %broadcast_multiply_fusion.6), kind=kLoop, calls=%fused_computation.4 | loop fusion | flops 8372224 | bytes 4325376 | tf_op jit(solution)/shard_map/reduce_sum | solution.py:98
  18.6 7.8 %fusion.22 = f32[64,256,128]{2,1,0:T(8,128)} fusion(bf16[64,256,128]{2,1,0:T(8,128)(2,1)S(1)} %copy-done.3, f32[128]{0:T(128)S(1)} %copy-done.2, f32[64,256]{1,0:T(8,128)S(1)} %add_rsqrt_fusion.1, f32[64,256]{1,0:T(8,128)S(1)} %broadcast_multiply_fusion.6, bf16[128,128]{1,0:T(8,128)(2,1)S(1)} %copy-done), kind=kOutput, calls=%fused_computation.41 | convolution fusion | flops 547356672 | bytes 12747264 | tf_op jit(solution)/shard_map/xkd,dh->hxk/dot_general | solution.py:155
  26.5 9.3 %copy.15 = f32[64,256,128]{1,0,2:T(8,128)} copy(f32[64,256,128]{2,1,0:T(8,128)} %fusion.22) | data formatting | bytes 16777216 | tf_op jit(solution)/shard_map/xkd,dh->hxk/dot_general | solution.py:155
  35.8 8.6 %fusion.20 = f32[64,256,128]{2,1,0:T(8,128)} fusion(bf16[64,256,128]{2,1,0:T(8,128)(2,1)} %param.10, f32[128]{0:T(128)S(1)} %copy-done.2, f32[64,256]{1,0:T(8,128)S(1)} %add_rsqrt_fusion.1, f32[64,256]{1,0:T(8,128)S(1)} %broadcast_multiply_fusion.6, bf16[128,128]{1,0:T(8,128)(2,1)S(1)} %copy-done.23), kind=kOutput, calls=%fused_computation.40 | convolution fusion | flops 547356672 | bytes 12747264 | tf_op jit(solution)/shard_map/xkd,dh->hxk/dot_general | solution.py:154
  44.4 9.3 %copy.16 = f32[64,256,128]{1,0,2:T(8,128)} copy(f32[64,256,128]{2,1,0:T(8,128)} %fusion.20) | data formatting | bytes 16777216 | tf_op jit(solution)/shard_map/xkd,dh->hxk/dot_general | solution.py:154
  56.6 8.7 %fusion.19.refs_7_.refs_5_ = bf16[128,64,256]{2,1,0:T(8,128)(2,1)} fusion(f32[64,256]{1,0:T(8,128)S(1)} %get-tuple-element.37, f32[64,256,128]{1,0,2:T(8,128)} %copy.16, f32[64,256,128]{1,0,2:T(8,128)} %copy.15), kind=kLoop, calls=%fused_computation.39 | loop fusion | flops 12582912 | bytes 21037056 | tf_op jit(solution)/shard_map/convert_element_type | solution.py:156
  67.9 30.7 %collective-permute-done.4.refs_1_ = bf16[32,256,128]{2,1,0:T(8,128)(2,1)} collective-permute-done((bf16[32,256,128]{2,1,0:T(8,128)(2,1)}, bf16[32,256,128]{2,1,0:T(8,128)(2,1)}, u32[]{:S(2)}, u32[]{:S(2)}) %collective-permute-start.4) | collective-permute-done | bytes 2097184 | tf_op jit(solution)/shard_map/ppermute | solution.py:135
  99.6 36.4 %shard_map.100 = f32[128,64,128]{2,1,0:T(8,128)} custom-call(s32[1]{0:T(128)} %bitcast.3.place_ref, bf16[32,256,128]{2,1,0:T(8,128)(2,1)S(1)} %get-tuple-element.19.refs_0_, bf16[32,256,128]{2,1,0:T(8,128)(2,1)} %get-tuple-element.20.refs_1_, bf16[32,256,128]{2,1,0:T(8,128)(2,1)} %collective-permute-done.refs_2_, ...), custom_call_target="tpu_custom_call" | custom-call | flops 42949672960 | bytes 20971520 | tf_op jit(solution)/shard_map/pallas_call | solution.py:69
  138.4 5.0 %collective-permute-done.3.refs_0_ = bf16[32,256,128]{2,1,0:T(8,128)(2,1)S(1)} collective-permute-done((bf16[32,256,128]{2,1,0:T(8,128)(2,1)}, bf16[32,256,128]{2,1,0:T(8,128)(2,1)S(1)}, u32[]{:S(2)}, u32[]{:S(2)}) %collective-permute-start.3) | collective-permute-done | bytes 2097184 | tf_op jit(solution)/shard_map/ppermute | solution.py:135
  144.4 44.0 %collective-permute-done.5.refs_1_ = bf16[32,256,128]{2,1,0:T(8,128)(2,1)} collective-permute-done((bf16[32,256,128]{2,1,0:T(8,128)(2,1)}, bf16[32,256,128]{2,1,0:T(8,128)(2,1)}, u32[]{:S(2)}, u32[]{:S(2)}) %collective-permute-start.5) | collective-permute-done | bytes 2097184 | tf_op jit(solution)/shard_map/ppermute | solution.py:135
  191.2 36.7 %shard_map.102 = f32[128,64,128]{2,1,0:T(8,128)} custom-call(s32[1]{0:T(128)} %bitcast.3.place_ref, bf16[32,256,128]{2,1,0:T(8,128)(2,1)} %collective-permute-done.2.refs_0_, bf16[32,256,128]{2,1,0:T(8,128)(2,1)} %collective-permute-done.4.refs_1_, bf16[32,256,128]{2,1,0:T(8,128)(2,1)} %copy-done.22, bf16[32,256,128]{2,1,0:T(8,128)(2,1)} %collective-permute-done.13.refs_3_, ...), custom_call_target="tpu_custom_call" | custom-call | flops 42949672960 | bytes 20971520 | tf_op jit(solution)/shard_map/pallas_call | solution.py:69
  227.9 50.5 %collective-permute-done.10.refs_1_ = bf16[32,256,128]{2,1,0:T(8,128)(2,1)} collective-permute-done((bf16[32,256,128]{2,1,0:T(8,128)(2,1)}, bf16[32,256,128]{2,1,0:T(8,128)(2,1)}, u32[]{:S(2)}, u32[]{:S(2)}) %collective-permute-start.10) | collective-permute-done | bytes 2097184 | tf_op jit(solution)/shard_map/ppermute | solution.py:135
  278.4 36.5 %shard_map.101 = f32[128,64,128]{2,1,0:T(8,128)} custom-call(s32[1]{0:T(128)} %bitcast.3.place_ref, bf16[32,256,128]{2,1,0:T(8,128)(2,1)S(1)} %collective-permute-done.3.refs_0_, bf16[32,256,128]{2,1,0:T(8,128)(2,1)} %collective-permute-done.5.refs_1_, bf16[32,256,128]{2,1,0:T(8,128)(2,1)} %collective-permute-done.6.refs_2_, ...), custom_call_target="tpu_custom_call" | custom-call | flops 42949672960 | bytes 20971520 | tf_op jit(solution)/shard_map/pallas_call | solution.py:69
  314.9 2.5 select_convert_fusion.1
  317.3 3.4 collective-permute-start.11
  326.5 22.4 %shard_map.103 = f32[128,64,64]{2,1,0:T(8,128)} custom-call(s32[1]{0:T(128)} %constant.114.clone.1.place_ref, bf16[32,256,128]{2,1,0:T(8,128)(2,1)S(1)} %collective-permute-done.9.refs_0_, bf16[32,256,128]{2,1,0:T(8,128)(2,1)} %collective-permute-done.10.refs_1_, f32[64,256]{1,0:T(8,128)S(1)} %get-tuple-element.35.refs_2_, f32[1,128]{1,0:T(1,128)S(1)} %bitcast.47, ...), custom_call_target="tpu_custom_call" | custom-call | flops 21474836480 | bytes 20971520 | tf_op jit(solution)/shard_map/pallas_call | solution.py:69
  348.9 3.3 fusion.41
  354.8 4.6 copy.27
  359.4 3.7 convert_reduce_fusion.2
  363.1 2.9 fusion.12
  366.1 2.4 fusion.24
  372.4 44.4 %collective-permute-done.15.refs_1_ = bf16[32,256,128]{2,1,0:T(8,128)(2,1)} collective-permute-done((bf16[32,256,128]{2,1,0:T(8,128)(2,1)}, bf16[32,256,128]{2,1,0:T(8,128)(2,1)}, u32[]{:S(2)}, u32[]{:S(2)}) %collective-permute-start.15) | collective-permute-done | bytes 2097184 | tf_op jit(solution)/shard_map/ppermute | solution.py:140
  416.8 23.0 %shard_map.104 = f32[128,64,64]{2,1,0:T(8,128)} custom-call(s32[1]{0:T(128)} %constant.114.clone.1.place_ref, bf16[32,256,128]{2,1,0:T(8,128)(2,1)} %collective-permute-done.14.refs_0_, bf16[32,256,128]{2,1,0:T(8,128)(2,1)} %collective-permute-done.15.refs_1_, f32[64,256]{1,0:T(8,128)S(1)} %get-tuple-element.36.refs_2_, f32[1,128]{1,0:T(1,128)S(1)} %bitcast.48, ...), custom_call_target="tpu_custom_call" | custom-call | flops 21474836480 | bytes 20971520 | tf_op jit(solution)/shard_map/pallas_call | solution.py:69
  439.8 3.9 broadcast_select_fusion.1
  443.7 3.0 select_convert_fusion
  459.3 6.7 %fusion.40 = (f32[64,128]{1,0:T(8,128)S(1)}, f32[128,64,128]{2,1,0:T(8,128)S(1)}) fusion(bf16[128,64,128]{2,1,0:T(8,128)(2,1)} %collective-permute-done.17, f32[128,64,128]{2,1,0:T(8,128)} %shard_map.102, f32[128,64,64]{2,1,0:T(8,128)} %copy-done.5, f32[128,64,64]{2,1,0:T(8,128)} %copy-done.4, pred[]{:T(512)S(6)} %eq.13), kind=kLoop, calls=%fused_computation.117 | loop fusion | flops 5234688 | bytes 14712833 | tf_op jit(solution)/shard_map/reduce_sum | solution.py:103
  467.2 3.4 copy.31
  470.6 3.7 convert_reduce_fusion.1
  474.4 3.0 fusion.9
  481.2 2.7 copy_dynamic-update-slice_fusion
  (137 shorter events, 47.1 us)
Async XLA Ops:
  0.0 18.6 %copy-start = (bf16[128,128]{1,0:T(8,128)(2,1)S(1)}, bf16[128,128]{1,0:T(8,128)(2,1)}, u32[]{:S(2)}) copy-start(bf16[128,128]{1,0:T(8,128)(2,1)} %param.16) | copy-start | bytes 98308
  4.0 61.3 %collective-permute-start.2 = (bf16[32,256,128]{2,1,0:T(8,128)(2,1)S(1)}, bf16[32,256,128]{2,1,0:T(8,128)(2,1)}, u32[]{:S(2)}, u32[]{:S(2)}) collective-permute-start(bf16[32,256,128]{2,1,0:T(8,128)(2,1)S(1)} %get-tuple-element.19.refs_0_), channel_id=1, source_target_pairs={{0,4},{2,6},{4,8},{6,10},{8,12},{10,14},{12,0},{14,2},{1,5},{3,7},... | collective-permute-start | bytes 6291464 | tf_op jit(solution)/shard_map/ppermute | solution.py:135
  6.2 92.4 %collective-permute-start = (bf16[32,256,128]{2,1,0:T(8,128)(2,1)S(1)}, bf16[32,256,128]{2,1,0:T(8,128)(2,1)}, u32[]{:S(2)}, u32[]{:S(2)}) collective-permute-start(bf16[32,256,128]{2,1,0:T(8,128)(2,1)S(1)} %get-tuple-element.19.refs_0_), channel_id=1, source_target_pairs={{0,2},{2,0},{4,6},{6,4},{8,10},{10,8},{12,14},{14,12},{1,3},{3,1},... | collective-permute-start | bytes 6291464 | tf_op jit(solution)/shard_map/ppermute | solution.py:140
  7.4 91.2 %collective-permute-start.4 = (bf16[32,256,128]{2,1,0:T(8,128)(2,1)}, bf16[32,256,128]{2,1,0:T(8,128)(2,1)}, u32[]{:S(2)}, u32[]{:S(2)}) collective-permute-start(bf16[32,256,128]{2,1,0:T(8,128)(2,1)} %get-tuple-element.20.refs_1_), channel_id=1, source_target_pairs={{0,4},{2,6},{4,8},{6,10},{8,12},{10,14},{12,0},{14,2},{1,5},{3,7},... | collective-permute-start | bytes 6291464 | tf_op jit(solution)/shard_map/ppermute | solution.py:135
  8.7 90.9 %collective-permute-start.1 = (bf16[32,256,128]{2,1,0:T(8,128)(2,1)}, bf16[32,256,128]{2,1,0:T(8,128)(2,1)}, u32[]{:S(2)}, u32[]{:S(2)}) collective-permute-start(bf16[32,256,128]{2,1,0:T(8,128)(2,1)} %get-tuple-element.20.refs_1_), channel_id=1, source_target_pairs={{0,2},{2,0},{4,6},{6,4},{8,10},{10,8},{12,14},{14,12},{1,3},{3,1},... | collective-permute-start | bytes 6291464 | tf_op jit(solution)/shard_map/ppermute | solution.py:140
  8.9 9.7 %copy-start.2 = (f32[128]{0:T(128)S(1)}, f32[128]{0:T(128)}, u32[]{:S(2)}) copy-start(f32[128]{0:T(128)} %param.12) | copy-start | bytes 1540
  26.5 9.3 %copy-start.23 = (bf16[128,128]{1,0:T(8,128)(2,1)S(1)}, bf16[128,128]{1,0:T(8,128)(2,1)}, u32[]{:S(2)}) copy-start(bf16[128,128]{1,0:T(8,128)(2,1)} %param.15) | copy-start | bytes 98308
  44.3 9.3 %copy-start.24 = (bf16[128,128]{1,0:T(8,128)(2,1)S(1)}, bf16[128,128]{1,0:T(8,128)(2,1)}, u32[]{:S(2)}) copy-start(bf16[128,128]{1,0:T(8,128)(2,1)} %param.13) | copy-start | bytes 98308
  44.3 9.4 %copy-start.25 = (bf16[128,128]{1,0:T(8,128)(2,1)S(1)}, bf16[128,128]{1,0:T(8,128)(2,1)}, u32[]{:S(2)}) copy-start(bf16[128,128]{1,0:T(8,128)(2,1)} %param.14) | copy-start | bytes 98308
  65.4 78.1 %collective-permute-start.3 = (bf16[32,256,128]{2,1,0:T(8,128)(2,1)}, bf16[32,256,128]{2,1,0:T(8,128)(2,1)S(1)}, u32[]{:S(2)}, u32[]{:S(2)}) collective-permute-start(bf16[32,256,128]{2,1,0:T(8,128)(2,1)} %collective-permute-done.2.refs_0_), channel_id=1, source_target_pairs={{0,4},{2,6},{4,8},{6,10},{8,12},{10,14},{12,0},{14,2},{1,5},{3,7},... | collective-permute-start | bytes 6291464 | tf_op jit(solution)/shard_map/ppermute | solution.py:135
  66.7 123.2 %collective-permute-start.12 = (bf16[32,256,128]{2,1,0:T(8,128)(2,1)}, bf16[32,256,128]{2,1,0:T(8,128)(2,1)S(1)}, u32[]{:S(2)}, u32[]{:S(2)}) collective-permute-start(bf16[32,256,128]{2,1,0:T(8,128)(2,1)} %collective-permute-done.2.refs_0_), channel_id=1, source_target_pairs={{0,2},{2,0},{4,6},{6,4},{8,10},{10,8},{12,14},{14,12},{1,3},{3,1},... | collective-permute-start | bytes 6291464 | tf_op jit(solution)/shard_map/ppermute | solution.py:140
  98.6 89.9 %collective-permute-start.5 = (bf16[32,256,128]{2,1,0:T(8,128)(2,1)}, bf16[32,256,128]{2,1,0:T(8,128)(2,1)}, u32[]{:S(2)}, u32[]{:S(2)}) collective-permute-start(bf16[32,256,128]{2,1,0:T(8,128)(2,1)} %collective-permute-done.4.refs_1_), channel_id=1, source_target_pairs={{0,4},{2,6},{4,8},{6,10},{8,12},{10,14},{12,0},{14,2},{1,5},{3,7},... | collective-permute-start | bytes 6291464 | tf_op jit(solution)/shard_map/ppermute | solution.py:135
  98.6 92.3 %collective-permute-start.13 = (bf16[32,256,128]{2,1,0:T(8,128)(2,1)}, bf16[32,256,128]{2,1,0:T(8,128)(2,1)}, u32[]{:S(2)}, u32[]{:S(2)}) collective-permute-start(bf16[32,256,128]{2,1,0:T(8,128)(2,1)} %collective-permute-done.4.refs_1_), channel_id=1, source_target_pairs={{0,2},{2,0},{4,6},{6,4},{8,10},{10,8},{12,14},{14,12},{1,3},{3,1},... | collective-permute-start | bytes 6291464 | tf_op jit(solution)/shard_map/ppermute | solution.py:140
  99.6 38.6 %copy-start.17 = (bf16[32,64,128]{2,1,0:T(8,128)(2,1)S(1)}, bf16[32,64,128]{2,1,0:T(8,128)(2,1)}, u32[]{:S(2)}) copy-start(bf16[32,64,128]{2,1,0:T(8,128)(2,1)} %get-tuple-element.41) | copy-start | bytes 1572868
  99.6 38.6 %copy-start.18 = (bf16[32,64,128]{2,1,0:T(8,128)(2,1)S(1)}, bf16[32,64,128]{2,1,0:T(8,128)(2,1)}, u32[]{:S(2)}) copy-start(bf16[32,64,128]{2,1,0:T(8,128)(2,1)} %get-tuple-element.42) | copy-start | bytes 1572868
  138.4 184.7 %copy-start.9 = (bf16[64,64,128]{2,1,0:T(8,128)(2,1)}, bf16[64,64,128]{2,1,0:T(8,128)(2,1)S(1)}, u32[]{:S(2)}) copy-start(bf16[64,64,128]{2,1,0:T(8,128)(2,1)S(1)} %get-tuple-element.26) | copy-start | bytes 3145732
  143.4 134.9 %collective-permute-start.9 = (bf16[32,256,128]{2,1,0:T(8,128)(2,1)S(1)}, bf16[32,256,128]{2,1,0:T(8,128)(2,1)S(1)}, u32[]{:S(2)}, u32[]{:S(2)}) collective-permute-start(bf16[32,256,128]{2,1,0:T(8,128)(2,1)S(1)} %collective-permute-done.3.refs_0_), channel_id=1, source_target_pairs={{0,4},{2,6},{4,8},{6,10},{8,12},{10,14},{12,0},{14,2},{1,5},{3,7},... | collective-permute-start | bytes 6291464 | tf_op jit(solution)/shard_map/ppermute | solution.py:135
  143.4 134.9 %collective-permute-start.6 = (bf16[32,256,128]{2,1,0:T(8,128)(2,1)S(1)}, bf16[32,256,128]{2,1,0:T(8,128)(2,1)}, u32[]{:S(2)}, u32[]{:S(2)}) collective-permute-start(bf16[32,256,128]{2,1,0:T(8,128)(2,1)S(1)} %collective-permute-done.3.refs_0_), channel_id=1, source_target_pairs={{0,2},{2,0},{4,6},{6,4},{8,10},{10,8},{12,14},{14,12},{1,3},{3,1},... | collective-permute-start | bytes 6291464 | tf_op jit(solution)/shard_map/ppermute | solution.py:140
  188.5 89.9 %collective-permute-start.10 = (bf16[32,256,128]{2,1,0:T(8,128)(2,1)}, bf16[32,256,128]{2,1,0:T(8,128)(2,1)}, u32[]{:S(2)}, u32[]{:S(2)}) collective-permute-start(bf16[32,256,128]{2,1,0:T(8,128)(2,1)} %collective-permute-done.5.refs_1_), channel_id=1, source_target_pairs={{0,4},{2,6},{4,8},{6,10},{8,12},{10,14},{12,0},{14,2},{1,5},{3,7},... | collective-permute-start | bytes 6291464 | tf_op jit(solution)/shard_map/ppermute | solution.py:135
  189.8 88.5 %collective-permute-start.7 = (bf16[32,256,128]{2,1,0:T(8,128)(2,1)}, bf16[32,256,128]{2,1,0:T(8,128)(2,1)}, u32[]{:S(2)}, u32[]{:S(2)}) collective-permute-start(bf16[32,256,128]{2,1,0:T(8,128)(2,1)} %collective-permute-done.5.refs_1_), channel_id=1, source_target_pairs={{0,2},{2,0},{4,6},{6,4},{8,10},{10,8},{12,14},{14,12},{1,3},{3,1},... | collective-permute-start | bytes 6291464 | tf_op jit(solution)/shard_map/ppermute | solution.py:140
  278.4 36.5 %copy-start.6 = (f32[128,64,128]{2,1,0:T(8,128)S(1)}, f32[128,64,128]{2,1,0:T(8,128)}, u32[]{:S(2)}) copy-start(f32[128,64,128]{2,1,0:T(8,128)} %shard_map.100) | copy-start | bytes 12582916
  317.3 31.6 %collective-permute-start.11 = (bf16[128,64,128]{2,1,0:T(8,128)(2,1)}, bf16[128,64,128]{2,1,0:T(8,128)(2,1)}, u32[]{:S(2)}, u32[]{:S(2)}) collective-permute-start(bf16[128,64,128]{2,1,0:T(8,128)(2,1)} %select_convert_fusion.1), channel_id=1, source_target_pairs={{0,1},{1,0},{2,3},{3,2},{4,5},{5,4},{6,7},{7,6},{8,9},{9,8},{10,11... | collective-permute-start | bytes 6291464 | tf_op jit(solution)/shard_map/ppermute | solution.py:143
  323.1 25.8 %copy-start.13 = (bf16[64,64,128]{2,1,0:T(8,128)(2,1)}, bf16[64,64,128]{2,1,0:T(8,128)(2,1)S(1)}, u32[]{:S(2)}) copy-start(bf16[64,64,128]{2,1,0:T(8,128)(2,1)S(1)} %get-tuple-element.27) | copy-start | bytes 3145732
  323.1 25.8 %copy-start.14 = (bf16[64,64,128]{2,1,0:T(8,128)(2,1)}, bf16[64,64,128]{2,1,0:T(8,128)(2,1)S(1)}, u32[]{:S(2)}) copy-start(bf16[64,64,128]{2,1,0:T(8,128)(2,1)S(1)} %get-tuple-element.28) | copy-start | bytes 3145732
  325.0 34.3 %collective-permute-start.8 = (bf16[128,64,128]{2,1,0:T(8,128)(2,1)}, bf16[128,64,128]{2,1,0:T(8,128)(2,1)}, u32[]{:S(2)}, u32[]{:S(2)}) collective-permute-start(bf16[128,64,128]{2,1,0:T(8,128)(2,1)} %broadcast_select_fusion.3), channel_id=1, source_target_pairs={{0,1},{1,0},{2,3},{3,2},{4,5},{5,4},{6,7},{7,6},{8,9},{9,8},{10,11... | collective-permute-start | bytes 6291464 | tf_op jit(solution)/shard_map/ppermute | solution.py:143
  325.0 47.4 %collective-permute-start.14 = (bf16[32,256,128]{2,1,0:T(8,128)(2,1)S(1)}, bf16[32,256,128]{2,1,0:T(8,128)(2,1)}, u32[]{:S(2)}, u32[]{:S(2)}) collective-permute-start(bf16[32,256,128]{2,1,0:T(8,128)(2,1)S(1)} %collective-permute-done.9.refs_0_), channel_id=1, source_target_pairs={{0,2},{2,0},{4,6},{6,4},{8,10},{10,8},{12,14},{14,12},{1,3},{3,1},... | collective-permute-start | bytes 6291464 | tf_op jit(solution)/shard_map/ppermute | solution.py:140
  326.3 90.5 %collective-permute-start.15 = (bf16[32,256,128]{2,1,0:T(8,128)(2,1)}, bf16[32,256,128]{2,1,0:T(8,128)(2,1)}, u32[]{:S(2)}, u32[]{:S(2)}) collective-permute-start(bf16[32,256,128]{2,1,0:T(8,128)(2,1)} %collective-permute-done.10.refs_1_), channel_id=1, source_target_pairs={{0,2},{2,0},{4,6},{6,4},{8,10},{10,8},{12,14},{14,12},{1,3},{3,1},... | collective-permute-start | bytes 6291464 | tf_op jit(solution)/shard_map/ppermute | solution.py:140
  326.5 22.4 %copy-start.7 = (f32[128,64,128]{2,1,0:T(8,128)S(1)}, f32[128,64,128]{2,1,0:T(8,128)}, u32[]{:S(2)}) copy-start(f32[128,64,128]{2,1,0:T(8,128)} %shard_map.101) | copy-start | bytes 12582916
  372.4 44.4 %copy-start.16 = (bf16[64,256,128]{2,1,0:T(8,128)(2,1)}, bf16[64,256,128]{2,1,0:T(8,128)(2,1)S(1)}, u32[]{:S(2)}) copy-start(bf16[64,256,128]{2,1,0:T(8,128)(2,1)S(1)} %copy_dynamic-update-slice_fusion.1) | copy-start | bytes 12582916
  416.8 23.0 %copy-start.15 = (f32[128,64,64]{2,1,0:T(8,128)S(1)}, f32[128,64,64]{2,1,0:T(8,128)}, u32[]{:S(2)}) copy-start(f32[128,64,64]{2,1,0:T(8,128)} %shard_map.103) | copy-start | bytes 6291460
  447.6 11.8 %collective-permute-start.17 = (bf16[128,64,128]{2,1,0:T(8,128)(2,1)}, bf16[128,64,128]{2,1,0:T(8,128)(2,1)}, u32[]{:S(2)}, u32[]{:S(2)}) collective-permute-start(bf16[128,64,128]{2,1,0:T(8,128)(2,1)} %select_convert_fusion), channel_id=1, source_target_pairs={{0,1},{1,0},{2,3},{3,2},{4,5},{5,4},{6,7},{7,6},{8,9},{9,8},{10,11... | collective-permute-start | bytes 6291464 | tf_op jit(solution)/shard_map/ppermute | solution.py:143
  459.3 11.3 %collective-permute-start.16 = (bf16[128,64,128]{2,1,0:T(8,128)(2,1)}, bf16[128,64,128]{2,1,0:T(8,128)(2,1)}, u32[]{:S(2)}, u32[]{:S(2)}) collective-permute-start(bf16[128,64,128]{2,1,0:T(8,128)(2,1)} %broadcast_select_fusion.2), channel_id=1, source_target_pairs={{0,1},{1,0},{2,3},{3,2},{4,5},{5,4},{6,7},{7,6},{8,9},{9,8},{10,11... | collective-permute-start | bytes 6291464 | tf_op jit(solution)/shard_map/ppermute | solution.py:143
  (15 other events, 75.6 us)
